TPU v7x, 128 devices: a whole 4x4x4 slice. The times are simulated.
128 devices in a mesh: ctx: 16 (over x_lo, z, core), tp: 8 (over y, x_hi).
Axes of the slice: x: 4 (x_hi: 2, x_lo: 2; x = x_hi * 2 + x_lo), y: 4, z: 4, core: 2. Of those that a mesh axis runs over, the one named last changes fastest.
Arguments:
- tokens: bfloat16 [16384, 1024], P(('ctx', 'tp')), may hold values from -6 to 6
- block_table: int32 [16, 2], replicated, may hold values from 0 to 31, as said below
- doc_ids: int32 [4, 4096], replicated, may hold values from 0 to 3, never falling along the last dimension, each value on 1 to 2048 neighbouring positions
- attn_gain: bfloat16 [1024], P('ctx'), may hold values from 0.25 to 1.75
- w_query: bfloat16 [1024, 2048], P('ctx', 'tp'), may hold values from -0.1875 to 0.1875
- w_key: bfloat16 [1024, 1024], P('ctx', 'tp'), may hold values from -0.1875 to 0.1875
- w_value: bfloat16 [1024, 1024], P('ctx', 'tp'), may hold values from -0.1875 to 0.1875
- query_gain: bfloat16 [128], P('ctx'), may hold values from 0.25 to 1.75
- key_gain: bfloat16 [128], P('ctx'), may hold values from 0.25 to 1.75
- w_out: bfloat16 [2048, 1024], P('tp', 'ctx'), may hold values from -1 to 1
- ffn_gain: bfloat16 [1024], P('ctx'), may hold values from 0.25 to 1.75
- w_gate: bfloat16 [1024, 3072], P('ctx', 'tp'), may hold values from -0.1875 to 0.1875
- w_up: bfloat16 [1024, 3072], P('ctx', 'tp'), may hold values from -0.1875 to 0.1875
- w_down: bfloat16 [3072, 1024], P('tp', 'ctx'), may hold values from -0.109375 to 0.109375
- out_grad: bfloat16 [16384, 1024], P(('ctx', 'tp')), may hold values from -6 to 6
Outputs:
- out: bfloat16 [16384, 1024], P(('ctx', 'tp'))
- grad_x: bfloat16 [16384, 1024], P(('ctx', 'tp'))
- grad_attn_gain: float32 [1024], P('ctx')
- grad_w_query: float32 [1024, 2048], P('ctx', 'tp')
- grad_w_key: float32 [1024, 1024], P('ctx', 'tp')
- grad_w_value: float32 [1024, 1024], P('ctx', 'tp')
- grad_query_gain: float32 [128], P('ctx')
- grad_key_gain: float32 [128], P('ctx')
- grad_w_out: float32 [2048, 1024], P('tp', 'ctx')
- grad_ffn_gain: float32 [1024], P('ctx')
- grad_w_gate: float32 [1024, 3072], P('ctx', 'tp')
- grad_w_up: float32 [1024, 3072], P('ctx', 'tp')
- grad_w_down: float32 [3072, 1024], P('tp', 'ctx')
Inputs may be any that keep to these rules, and one draw needn't show every extreme that they name: `block_table`: row c holds a block b below 16 and its mirror 2 * 16 - 1 - b; the first entries of the rows form a permutation, so every block appears once. `doc_ids`: never falling along a row; each document has 1 to 2048 positions, one exactly that many.
All inputs are finite; a program needn't handle non-finite values.
Results may differ from a plain program's by a relative error of at most 0.025.
Values may be sent and summed in bfloat16 or wider, within the bound.
No kernel may reach another device: no remote copies, remote signals or barrier semaphores. Data moves between devices by JAX's collectives and lax.ppermute only.
A program may use at most 192 MiB of HBM per device.

v0:
```python
import math

import jax
import jax.numpy as jnp
from jax import lax
from jax.sharding import PartitionSpec as P

HD = 128


EPS = 1e-06
THETA = 1000000.0
NEG_SCORE = -1e30


def split_up(shard, dim, length):
    before, after = (shard.shape[:dim], shard.shape[dim + 1 :])
    return jnp.moveaxis(shard.reshape(*before, length, -1, *after), dim, 0)


def sent_and_summed(shard, axis, dim):
    parts = split_up(shard, dim, lax.axis_size(axis))
    arrived = lax.all_to_all(parts, axis, split_axis=0, concat_axis=0, tiled=True)
    return arrived.astype(jnp.float32).sum(axis=0)


def normed(values, norm_gain):
    return values * lax.rsqrt(jnp.mean(values * values, axis=-1, keepdims=True) + EPS) * norm_gain


def rotate(values, cos_table, sin_table):
    half_width = values.shape[-1] // 2
    turned = jnp.concatenate([-values[..., half_width:], values[..., :half_width]], axis=-1)
    return values * cos_table + turned * sin_table


def contract_last(left_side, right_side):
    return lax.dot_general(
        left_side, right_side, (((1,), (1,)), ((), ())), preferred_element_type=jnp.float32
    )


def contract_first(left_side, right_side):
    return lax.dot_general(
        left_side, right_side, (((0,), (0,)), ((), ())), preferred_element_type=jnp.float32
    )


def send_grads(stacked):
    return lax.psum_scatter(
        stacked.astype(jnp.bfloat16), "ctx", scatter_dimension=0, tiled=True
    ).astype(jnp.float32)


def per_device(
    tokens,
    block_table,
    doc_ids,
    attn_gain,
    w_query,
    w_key,
    w_value,
    query_gain,
    key_gain,
    w_out,
    ffn_gain,
    w_gate,
    w_up,
    w_down,
    out_grad,
):
    ctx_count = lax.axis_size("ctx")
    tp_count = lax.axis_size("tp")
    ctx_rank = lax.axis_index("ctx")
    rows_dev = tokens.shape[0]
    local_rows = rows_dev * tp_count
    seq_count = doc_ids.shape[0]
    pair_rows = local_rows // seq_count
    seq_keys = pair_rows * ctx_count
    q_heads = w_query.shape[1] // HD
    kv_heads = w_key.shape[1] // HD
    group_size = q_heads // kv_heads
    q_width = q_heads * HD
    k_width = kv_heads * HD
    ff_local = w_gate.shape[1]
    score_scale = HD ** (-0.5)
    key_block = math.gcd(seq_keys, 512)
    key_blocks = seq_keys // key_block
    seq_len = doc_ids.shape[1]
    half_block = pair_rows // 2
    seq_index = jnp.arange(seq_len, dtype=jnp.int32)
    change = jnp.concatenate(
        [jnp.ones((seq_count, 1), dtype=bool), doc_ids[:, 1:] != doc_ids[:, :-1]], axis=1
    )
    doc_starts = lax.cummax(jnp.where(change, seq_index[None, :], 0), axis=1)
    key_index = jnp.arange(seq_keys, dtype=jnp.int32)
    key_inner = key_index % pair_rows
    key_place = (
        block_table[key_index // pair_rows, key_inner // half_block] * half_block
        + key_inner % half_block
    )
    key_doc = doc_ids[:, key_place]
    query_index = jnp.arange(local_rows, dtype=jnp.int32)
    query_seq = query_index // pair_rows
    query_inner = query_index % pair_rows
    query_place = (
        block_table[jnp.zeros_like(query_index) + ctx_rank, query_inner // half_block] * half_block
        + query_inner % half_block
    )
    query_doc = doc_ids[query_seq, query_place]
    query_pos = query_place - doc_starts[query_seq, query_place]
    query_place_s = query_place.reshape(seq_count, pair_rows)
    query_doc_s = query_doc.reshape(seq_count, pair_rows)
    freq_steps = jnp.arange(HD // 2, dtype=jnp.float32) * (2.0 / HD)
    angles = (
        query_pos.astype(jnp.float32)[:, None] * jnp.power(jnp.float32(THETA), -freq_steps)[None, :]
    )
    angles = jnp.concatenate([angles, angles], axis=1)[:, None, :]
    cos_table = jnp.cos(angles)
    sin_table = jnp.sin(angles)
    gain_attn, gain_query, gain_key, w_qkv, w_proj = (
        lax.all_gather(attn_gain, "ctx", axis=0, tiled=True),
        lax.all_gather(query_gain, "ctx", axis=0, tiled=True),
        lax.all_gather(key_gain, "ctx", axis=0, tiled=True),
        lax.all_gather(
            jnp.concatenate([w_query, w_key, w_value], axis=1), "ctx", axis=0, tiled=True
        ),
        lax.all_gather(w_out, "ctx", axis=1, tiled=True),
    )
    tokens_f = tokens.astype(jnp.float32)
    normal_one_f, norm_one_back = jax.vjp(normed, tokens_f, gain_attn.astype(jnp.float32))
    normal_one = normal_one_f.astype(jnp.bfloat16)
    rows_one = lax.all_gather(normal_one, "tp", axis=0, tiled=True)
    projected = jnp.dot(rows_one, w_qkv, preferred_element_type=jnp.float32)
    query_pre = projected[:, :q_width].reshape(local_rows, q_heads, HD)
    key_pre = projected[:, q_width : q_width + k_width].reshape(local_rows, kv_heads, HD)
    value_low = projected[:, q_width + k_width :].astype(jnp.bfloat16)

    def head_prep(pre_values, norm_gain):
        return rotate(normed(pre_values, norm_gain), cos_table, sin_table)

    query_rot, query_back = jax.vjp(head_prep, query_pre, gain_query.astype(jnp.float32))
    key_rot, key_back = jax.vjp(head_prep, key_pre, gain_key.astype(jnp.float32))
    query_low = query_rot.astype(jnp.bfloat16).reshape(
        seq_count, pair_rows, kv_heads, group_size, HD
    )
    key_low = key_rot.astype(jnp.bfloat16).reshape(seq_count, pair_rows, k_width)
    own_values = value_low.reshape(seq_count, pair_rows, k_width)
    keys_all, values_all = (
        lax.all_gather(key_low, "ctx", axis=1, tiled=True),
        lax.all_gather(own_values, "ctx", axis=1, tiled=True),
    )
    keys_seq = keys_all.reshape(seq_count, seq_keys, kv_heads, HD)
    values_seq = values_all.reshape(seq_count, seq_keys, kv_heads, HD)

    def tile_at(start):
        key_tile = lax.dynamic_slice_in_dim(keys_seq, start, key_block, 1)
        value_tile = lax.dynamic_slice_in_dim(values_seq, start, key_block, 1)
        place_tile = lax.dynamic_slice_in_dim(key_place, start, key_block, 0)
        doc_tile = lax.dynamic_slice_in_dim(key_doc, start, key_block, 1)
        scores = (
            jnp.einsum("sqhgd,skhd->shgqk", query_low, key_tile, preferred_element_type=jnp.float32)
            * score_scale
        )
        allowed = (doc_tile[:, None, :] == query_doc_s[:, :, None]) & (
            place_tile[None, None, :] <= query_place_s[:, :, None]
        )
        return (key_tile, value_tile, scores, allowed[:, None, None, :, :])

    starts = jnp.arange(key_blocks, dtype=jnp.int32) * key_block

    def stats_step(running, start):
        peak_score, row_total = running
        key_tile, value_tile, scores, allowed = tile_at(start)
        scores = jnp.where(allowed, scores, NEG_SCORE)
        new_peak = jnp.maximum(peak_score, jnp.max(scores, axis=-1))
        weights = jnp.where(allowed, jnp.exp(scores - new_peak[..., None]), 0.0)
        row_total = row_total * jnp.exp(peak_score - new_peak) + jnp.sum(weights, axis=-1)
        return ((new_peak, row_total), None)

    stat_shape = (seq_count, kv_heads, group_size, pair_rows)
    stats_final = lax.scan(
        stats_step,
        (jnp.full(stat_shape, NEG_SCORE, jnp.float32), jnp.zeros(stat_shape, jnp.float32)),
        starts,
    )[0]
    log_total = stats_final[0] + jnp.log(stats_final[1])

    def output_step(accum, start):
        key_tile, value_tile, scores, allowed = tile_at(start)
        probs_low = jnp.where(allowed, jnp.exp(scores - log_total[..., None]), 0.0).astype(
            jnp.bfloat16
        )
        return (
            accum
            + jnp.einsum(
                "shgqk,skhd->sqhgd", probs_low, value_tile, preferred_element_type=jnp.float32
            ),
            None,
        )

    head_shape = (seq_count, pair_rows, kv_heads, group_size, HD)
    attended = lax.scan(output_step, jnp.zeros(head_shape, jnp.float32), starts)[0]
    attn_low = attended.reshape(local_rows, q_width).astype(jnp.bfloat16)
    resid = tokens_f + lax.psum_scatter(
        jnp.dot(attn_low, w_proj, preferred_element_type=jnp.float32).astype(jnp.bfloat16),
        "tp",
        scatter_dimension=0,
        tiled=True,
    ).astype(jnp.float32)
    gain_ffn, w_gu, w_dn = (
        lax.all_gather(ffn_gain, "ctx", axis=0, tiled=True),
        lax.all_gather(jnp.concatenate([w_gate, w_up], axis=1), "ctx", axis=0, tiled=True),
        lax.all_gather(w_down, "ctx", axis=1, tiled=True),
    )
    normal_two_f, norm_two_back = jax.vjp(normed, resid, gain_ffn.astype(jnp.float32))
    normal_two = normal_two_f.astype(jnp.bfloat16)
    rows_two = lax.all_gather(normal_two, "tp", axis=0, tiled=True)
    gate_up = jnp.dot(rows_two, w_gu, preferred_element_type=jnp.float32)
    gate = gate_up[:, :ff_local]
    up_proj = gate_up[:, ff_local:]
    sigmoid_gate = jax.nn.sigmoid(gate)
    silu_gate = gate * sigmoid_gate
    hidden = (silu_gate * up_proj).astype(jnp.bfloat16)
    out = (
        resid
        + sent_and_summed(
            jnp.dot(hidden, w_dn, preferred_element_type=jnp.float32).astype(jnp.bfloat16), "tp", 0
        )
    ).astype(jnp.bfloat16)
    grad_rows = lax.all_gather(out_grad, "tp", axis=0, tiled=True)
    grad_hidden = contract_last(grad_rows, w_dn)
    grad_gate = grad_hidden * up_proj * (sigmoid_gate * (1.0 + gate * (1.0 - sigmoid_gate)))
    grad_up = grad_hidden * silu_gate
    grad_gu = jnp.concatenate([grad_gate, grad_up], axis=1).astype(jnp.bfloat16)
    mlp_grads = jnp.concatenate(
        [contract_first(rows_two, grad_gu), contract_first(grad_rows, hidden)], axis=1
    )
    mlp_early = send_grads(mlp_grads)
    grad_norm_two = sent_and_summed(contract_last(grad_gu, w_gu).astype(jnp.bfloat16), "tp", 0)
    grad_resid_norm, grad_gain_ffn = norm_two_back(grad_norm_two)
    grad_resid = out_grad.astype(jnp.float32) + grad_resid_norm
    branch_rows = lax.all_gather(grad_resid.astype(jnp.bfloat16), "tp", axis=0, tiled=True)
    grad_attn_low = contract_last(branch_rows, w_proj).astype(jnp.bfloat16)
    grad_out_cols = contract_first(branch_rows, attn_low)
    grad_attn_heads = grad_attn_low.reshape(head_shape)
    delta = jnp.transpose(
        jnp.sum(grad_attn_heads.astype(jnp.float32) * attended, axis=-1), (0, 2, 3, 1)
    )

    def scores_grad(probs, grad_probs, delta_here):
        return (probs * (grad_probs - delta_here[..., None])).astype(jnp.bfloat16)

    def grad_step(carry, start):
        accum, key_grad_all, value_grad_all = carry
        key_tile, value_tile, scores, allowed = tile_at(start)
        probs = jnp.where(allowed, jnp.exp(scores - log_total[..., None]), 0.0)
        probs_low = probs.astype(jnp.bfloat16)
        grad_value = jnp.einsum(
            "shgqk,sqhgd->skhd", probs_low, grad_attn_heads, preferred_element_type=jnp.float32
        )
        grad_probs = jnp.einsum(
            "sqhgd,skhd->shgqk", grad_attn_heads, value_tile, preferred_element_type=jnp.float32
        )
        grad_scores = scores_grad(probs, grad_probs, delta)
        accum = (
            accum
            + jnp.einsum(
                "shgqk,skhd->sqhgd", grad_scores, key_tile, preferred_element_type=jnp.float32
            )
            * score_scale
        )
        grad_key = (
            jnp.einsum(
                "shgqk,sqhgd->skhd", grad_scores, query_low, preferred_element_type=jnp.float32
            )
            * score_scale
        )
        key_grad_all = lax.dynamic_update_slice_in_dim(
            key_grad_all, grad_key.reshape(seq_count, key_block, k_width), start, 1
        )
        value_grad_all = lax.dynamic_update_slice_in_dim(
            value_grad_all, grad_value.reshape(seq_count, key_block, k_width), start, 1
        )
        return ((accum, key_grad_all, value_grad_all), None)

    kv_zero = jnp.zeros((seq_count, seq_keys, k_width), jnp.float32)
    grad_query, key_grad_all, value_grad_all = lax.scan(
        grad_step, (jnp.zeros(head_shape, jnp.float32), kv_zero, kv_zero), starts
    )[0]
    grad_keys, grad_values = (
        lax.psum_scatter(
            key_grad_all.astype(jnp.bfloat16), "ctx", scatter_dimension=1, tiled=True
        ).astype(jnp.float32),
        lax.psum_scatter(
            value_grad_all.astype(jnp.bfloat16), "ctx", scatter_dimension=1, tiled=True
        ).astype(jnp.float32),
    )
    grad_query_pre, grad_gain_query = query_back(grad_query.reshape(local_rows, q_heads, HD))
    grad_key_pre, grad_gain_key = key_back(grad_keys.reshape(local_rows, kv_heads, HD))
    grad_qkv = jnp.concatenate(
        [
            grad_query_pre.reshape(local_rows, q_width),
            grad_key_pre.reshape(local_rows, k_width),
            grad_values.reshape(local_rows, k_width),
        ],
        axis=1,
    ).astype(jnp.bfloat16)
    attn_grads = jnp.concatenate([contract_first(rows_one, grad_qkv), grad_out_cols], axis=1)
    grad_norm_one = sent_and_summed(contract_last(grad_qkv, w_qkv).astype(jnp.bfloat16), "tp", 0)
    grad_input_norm, grad_gain_attn = norm_one_back(grad_norm_one)
    grad_x = (grad_resid + grad_input_norm).astype(jnp.bfloat16)
    gain_sums = lax.psum(
        (grad_gain_attn, grad_gain_query, grad_gain_key, grad_gain_ffn), ("ctx", "tp")
    )
    d_share = gain_sums[0].shape[0] // ctx_count
    h_share = gain_sums[1].shape[0] // ctx_count
    attn_owned = send_grads(attn_grads)
    return (
        out,
        grad_x,
        lax.dynamic_slice_in_dim(gain_sums[0], ctx_rank * d_share, d_share),
        attn_owned[:, :q_width],
        attn_owned[:, q_width : q_width + k_width],
        attn_owned[:, q_width + k_width : q_width + 2 * k_width],
        lax.dynamic_slice_in_dim(gain_sums[1], ctx_rank * h_share, h_share),
        lax.dynamic_slice_in_dim(gain_sums[2], ctx_rank * h_share, h_share),
        jnp.transpose(attn_owned[:, q_width + 2 * k_width :]),
        lax.dynamic_slice_in_dim(gain_sums[3], ctx_rank * d_share, d_share),
        mlp_early[:, :ff_local],
        mlp_early[:, ff_local : 2 * ff_local],
        jnp.transpose(mlp_early[:, 2 * ff_local :]),
    )


def solution(mesh):
    in_specs = (
        P(("ctx", "tp"), None),
        P(),
        P(),
        P("ctx"),
        P("ctx", "tp"),
        P("ctx", "tp"),
        P("ctx", "tp"),
        P("ctx"),
        P("ctx"),
        P("tp", "ctx"),
        P("ctx"),
        P("ctx", "tp"),
        P("ctx", "tp"),
        P("tp", "ctx"),
        P(("ctx", "tp"), None),
    )
    out_specs = (
        P(("ctx", "tp"), None),
        P(("ctx", "tp"), None),
        P("ctx"),
        P("ctx", "tp"),
        P("ctx", "tp"),
        P("ctx", "tp"),
        P("ctx"),
        P("ctx"),
        P("tp", "ctx"),
        P("ctx"),
        P("ctx", "tp"),
        P("ctx", "tp"),
        P("tp", "ctx"),
    )
    return jax.shard_map(
        per_device, mesh=mesh, in_specs=in_specs, out_specs=out_specs, check_vma=False
    )
```

profile of v0, /device:TPU:1, one launch (start us, length us, event | category | flops | bytes accessed | tf_op | source)
XLA Modules:
  0.0 1123.9 jit_solution(7905820449707120170)
XLA Ops:
  14.7 30.3 %all-reduce.11 = (bf16[1024]{0:T(1024)(128)(2,1)S(1)}, bf16[128]{0:T(256)(128)(2,1)S(1)}, bf16[128]{0:T(256)(128)(2,1)S(1)}, bf16[1024]{0:T(1024)(128)(2,1)}) all-reduce(bf16[1024]{0:T(1024)(128)(2,1)S(1)} %dynamic-update-slice, bf16[128]{0:T(256)(128)(2,1)S(1)} %dynamic-update-slice.1, ...), channel_id=1, replica_groups=mesh['ctx'=16,'tp'=8] {'ctx'}, use_global_device_ids=true, to_apply=%add.6 | all-reduce | flops 2304 | bytes 9216
  52.0 8.8 gather_fusion.2
  60.9 9.1 gather_fusion.4
  70.9 33.8 %all-gather.9.cloned.1.call-done = bf16[1024,1024]{1,0:T(8,128)(2,1)} async-done(((bf16[128,1024]{1,0:T(8,128)(2,1)}), bf16[1024,1024]{1,0:T(8,128)(2,1)}) %all-gather.9.cloned.1.call-update) | async-done | bytes 2097168 | tf_op jit(solution)/shard_map/all_gather | solution.py:133
  104.7 3.1 fusion.161
  108.1 3.0 fusion.97
  112.1 9.1 gather_fusion.3
  124.0 33.8 %gather_fusion = s32[4096]{0:T(1024)S(1)} fusion(s32[16,2]{0,1:T(2,128)S(1)} %copy-done, s32[4096]{0:T(1024)S(1)} %bitcast.382), kind=kCustom, calls=%fused_computation | custom fusion | bytes 65536 | tf_op jit(solution)/shard_map/gather | solution.py:99
  157.9 15.8 %gather_fusion.1 = s32[4096,4]{1,0:T(8,128)} fusion(s32[4,4096]{0,1:T(8,128)} %copy.155, s32[4096]{0:T(1024)S(1)} %broadcast_clamp_fusion), kind=kCustom, calls=%fused_computation.1 | custom fusion | bytes 147456 | tf_op jit(solution)/shard_map/gather | solution.py:102
  176.6 4.9 fusion.109
  181.5 22.6 %all_gather.49 = bf16[256,1024]{0,1:T(8,128)(2,1)} all-gather(bf16[256,64]{0,1:T(8,128)(2,1)S(1)} %copy-done.40), channel_id=1, replica_groups=mesh['ctx'=16,'tp'=8] {'ctx'}, dimensions={1}, use_global_device_ids=true | all-gather | bytes 557056 | tf_op jit(solution)/shard_map/all_gather | solution.py:128
  213.9 56.3 %while.42 = (s32[]{:T(128)}, f32[4,1,2,256]{3,2,0,1:T(2,128)S(1)}, f32[4,1,2,256]{3,2,0,1:T(2,128)S(1)}, s32[8]{0:T(128)}, s32[4,4096]{1,0:T(4,128)S(1)}, /*inde...) while((s32[]{:T(128)}, f32[4,1,2,256]{3,2,0,1:T(2,128)S(1)}, ...), condition=%wide.wide.region_8.9_spmd.clone, body=%wide.wide.region_5.8_spmd.clone.sunk | while | flops 278407168 | bytes 11155674 | solution.py:182
  270.2 54.3 %while.43 = (s32[]{:T(128)}, f32[4,256,1,2,128]{1,4,3,0,2:T(8,128)S(1)}, s32[8]{0:T(128)}, bf16[4,4096,1,128]{3,1,0,2:T(8,128)(2,1)}, s32[4,4096]{1,0:T(4,128)S(...) while((s32[]{:T(128)}, ...), condition=%wide.wide.region_10.11_spmd.clone, body=%wide.wide.region_9.10_spmd.clone.sunk | while | flops 543162368 | bytes 4767452 | solution.py:203
  274.2 2.8 fusion.228
  281.0 2.8 fusion.228
  287.7 2.8 fusion.228
  294.5 2.8 fusion.228
  301.3 2.8 fusion.228
  308.1 2.8 fusion.228
  314.9 2.8 fusion.228
  321.7 2.8 fusion.228
  328.5 68.5 %reduce-scatter.10.cloned.1.call-done = bf16[128,1024]{1,0:T(8,128)(2,1)} async-done(((bf16[1024,1024]{1,0:T(8,128)(2,1)}), bf16[128,1024]{1,0:T(8,128)(2,1)}) %reduce-scatter.10.cloned.1.call-update) | async-done | bytes 262160 | tf_op jit(solution)/shard_map/reduce_scatter | solution.py:205
  400.8 24.0 %all_gather.53 = bf16[384,1024]{0,1:T(8,128)(2,1)S(1)} all-gather(bf16[384,64]{0,1:T(8,128)(2,1)} %param.34), channel_id=1, replica_groups=mesh['ctx'=16,'tp'=8] {'ctx'}, dimensions={1}, use_global_device_ids=true | all-gather | bytes 835584 | tf_op jit(solution)/shard_map/all_gather | solution.py:214
  424.8 9.0 all-gather.19.cloned.1.call-done
  433.8 55.6 %all-gather.17.cloned.1.call-done = bf16[1024,1024]{1,0:T(8,128)(2,1)} async-done(((bf16[128,1024]{1,0:T(8,128)(2,1)}), bf16[1024,1024]{1,0:T(8,128)(2,1)}) %all-gather.17.cloned.1.call-update) | async-done | bytes 2097168 | tf_op jit(solution)/shard_map/all_gather | solution.py:218
  489.4 5.5 fusion.162
  494.9 48.6 %all-gather.21.cloned.1.call-done = bf16[1024,1024]{1,0:T(8,128)(2,1)} async-done(((bf16[128,1024]{1,0:T(8,128)(2,1)}), bf16[1024,1024]{1,0:T(8,128)(2,1)}) %all-gather.21.cloned.1.call-update) | async-done | bytes 2097168 | tf_op jit(solution)/shard_map/all_gather | solution.py:231
  543.5 5.2 multiply_convert_fusion.1
  550.6 30.1 %all_to_all.15 = bf16[8,128,1024]{2,1,0:T(8,128)(2,1)S(1)} all-to-all(bf16[8,128,1024]{2,1,0:T(8,128)(2,1)S(1)} %bitcast.393), channel_id=1, replica_groups=mesh['ctx'=16,'tp'=8] {'tp'}, dimensions={0} | all-to-all | bytes 4194304 | tf_op jit(solution)/shard_map/all_to_all | solution.py:23
  583.5 52.6 %all-gather.23.cloned.1.call-done = bf16[1024,1024]{1,0:T(8,128)(2,1)} async-done(((bf16[128,1024]{1,0:T(8,128)(2,1)}), bf16[1024,1024]{1,0:T(8,128)(2,1)}) %all-gather.23.cloned.1.call-update) | async-done | bytes 2097168 | tf_op jit(solution)/shard_map/all_gather | solution.py:243
  636.2 3.1 convolution_convert_fusion.8
  646.1 2.6 broadcast_in_dim.107
  648.7 176.8 %while.44 = (s32[]{:T(128)}, f32[4,256,1,2,128]{1,4,3,0,2:T(8,128)S(1)}, bf16[4,4096,128]{2,1,0:T(8,128)(2,1)}, bf16[4,4096,128]{2,1,0:T(8,128)(2,1)}, s32[8]{0:...) while((s32[]{:T(128)}, ...), condition=%wide.wide.region_18.19_spmd.clone, body=%wide.wide.region_17.18_spmd.clone.sunk | while | flops 1355546624 | bytes 29423888 | solution.py:288
  654.8 2.5 fusion.240
  659.8 5.6 dynamic_update_slice.12
  665.4 5.6 dynamic_update_slice.13
  677.1 2.5 fusion.240
  682.1 5.6 dynamic_update_slice.12
  687.7 5.5 dynamic_update_slice.13
  699.4 2.5 fusion.240
  704.3 5.6 dynamic_update_slice.12
  709.9 5.6 dynamic_update_slice.13
  726.6 5.6 dynamic_update_slice.12
  732.2 5.6 dynamic_update_slice.13
  743.9 2.5 fusion.240
  748.9 5.6 dynamic_update_slice.12
  754.4 5.5 dynamic_update_slice.13
  771.1 5.6 dynamic_update_slice.12
  776.7 5.6 dynamic_update_slice.13
  793.4 5.6 dynamic_update_slice.12
  799.0 5.6 dynamic_update_slice.13
  815.6 4.9 dynamic_update_slice.12
  820.6 4.9 dynamic_update_slice.13
  826.7 2.7 fusion.80
  832.9 4.4 copy.197
  838.4 2.7 convolution_convert_fusion
  841.1 4.4 all-to-all-start
  854.6 41.9 %reduce-scatter.14.cloned.1.call-done = bf16[4,256,128]{2,1,0:T(8,128)(2,1)} async-done(((bf16[4,4096,128]{2,1,0:T(8,128)(2,1)}), bf16[4,256,128]{2,1,0:T(8,128)(2,1)}) %reduce-scatter.14.cloned.1.call-update) | async-done | bytes 262160 | tf_op jit(solution)/shard_map/reduce_scatter | solution.py:295
  897.6 64.9 %reduce-scatter.12.cloned.1.call-done = bf16[4,256,128]{2,1,0:T(8,128)(2,1)} async-done(((bf16[4,4096,128]{2,1,0:T(8,128)(2,1)}), bf16[4,256,128]{2,1,0:T(8,128)(2,1)}) %reduce-scatter.12.cloned.1.call-update) | async-done | bytes 262160 | tf_op jit(solution)/shard_map/reduce_scatter | solution.py:292
  972.7 3.9 convolution_convert_fusion.1
  976.6 6.5 all-to-all-start.2
  983.1 2.8 convert_reduce_fusion.2
  985.9 45.9 %reduce-scatter.18.cloned.1.call-done = bf16[64,1152]{1,0:T(8,128)(2,1)} async-done(((bf16[1024,1152]{1,0:T(8,128)(2,1)}), bf16[64,1152]{1,0:T(8,128)(2,1)}) %reduce-scatter.18.cloned.1.call-update) | async-done | bytes 147472
  1040.2 68.2 %all-reduce.10 = (f32[1024]{0:T(1024)S(1)}, f32[128]{0:T(128)S(1)}, f32[128]{0:T(128)S(1)}, f32[1024]{0:T(1024)S(1)}) all-reduce(f32[1024]{0:T(1024)S(1)} %get-tuple-element.576, f32[128]{0:T(128)S(1)} %get-tuple-element.574, f32[128]{0:T(128)S(1)} %get-tuple-element.570, ...), channel_id=1, replica_groups=mesh['ctx'=16,'tp'=8] {'ctx','tp'}, use_global_device_ids=true, to_apply=%region_26.27 | all-reduce | flops 2304 | bytes 18432 | tf_op jit(solution)/shard_map/psum | solution.py:313
  (461 shorter events, 211.5 us)
Async XLA Ops:
  7.2 44.9 %copy-start = (s32[16,2]{0,1:T(2,128)S(1)}, s32[16,2]{0,1:T(2,128)}, u32[]{:S(2)}) copy-start(s32[16,2]{0,1:T(2,128)} %param.22) | copy-start | bytes 388
  7.2 63.7 %all-gather.11.cloned.1.call-start = ((), (), s32[]{:S(2)}) async-start(), calls=%async_computation.9 | async-start | bytes 1114112 | tf_op jit(solution)/shard_map/all_gather | solution.py:125
  8.7 96.0 %all-gather.9.cloned.1.call-start = ((), (), s32[]{:S(2)}) async-start(), calls=%async_computation.8 | async-start | bytes 2359296 | tf_op jit(solution)/shard_map/all_gather | solution.py:133
  49.0 164.8 %all-gather.15.cloned.1.call-start = ((), (), s32[]{:S(2)}) async-start(), calls=%async_computation.11 | async-start | bytes 4456448 | tf_op jit(solution)/shard_map/all_gather | solution.py:150
  49.1 59.0 %copy-start.41 = (f32[128]{0:T(128)}, f32[128]{0:T(128)S(1)}, u32[]{:S(2)}) copy-start(f32[128]{0:T(128)S(1)} %convert_element_type.135) | copy-start | bytes 1540
  70.1 51.2 %copy-start.32 = (s32[1024]{0:T(1024)}, s32[1024]{0:T(1024)S(1)}, u32[]{:S(2)}) copy-start(s32[1024]{0:T(1024)S(1)} %get-tuple-element.1194) | copy-start | bytes 12292
  107.8 99.0 %copy-start.3 = (f32[1024,512]{0,1:T(8,128)}, f32[1024,512]{0,1:T(8,128)S(1)}, u32[]{:S(2)}) copy-start(f32[1024,512]{0,1:T(8,128)S(1)} %fusion.161) | copy-start | bytes 6291460
  107.9 3.2 copy-start.38
  108.1 4.0 copy-start.2
  112.0 158.2 %all-gather.13.cloned.1.call-start = ((), (), s32[]{:S(2)}) async-start(), calls=%async_computation.10 | async-start | bytes 4456448 | tf_op jit(solution)/shard_map/all_gather | solution.py:151
  121.2 36.6 %copy-start.34 = (s32[1024]{0:T(1024)}, s32[1024]{0:T(1024)S(1)}, u32[]{:S(2)}) copy-start(s32[1024]{0:T(1024)S(1)} %gather_fusion.3) | copy-start | bytes 12292
  157.9 23.7 %copy-start.40 = (bf16[256,64]{0,1:T(8,128)(2,1)S(1)}, bf16[256,64]{0,1:T(8,128)(2,1)}, u32[]{:S(2)}) copy-start(bf16[256,64]{0,1:T(8,128)(2,1)} %param.30) | copy-start | bytes 98308
  204.3 2.8 copy-start.6
  204.3 2.6 copy-start.43
  207.1 3.7 copy-start.14
  207.1 3.7 copy-start.22
  207.1 3.7 copy-start.23
  213.6 183.5 %reduce-scatter.10.cloned.1.call-start = ((), (), s32[]{:S(2)}) async-start(), calls=%async_computation.12 | async-start | bytes 2359296 | tf_op jit(solution)/shard_map/reduce_scatter | solution.py:205
  213.9 56.3 %copy-start.13 = (f32[4,256,1,2,128]{1,4,3,0,2:T(8,128)S(1)}, f32[4,256,1,2,128]{1,4,3,0,2:T(8,128)}, u32[]{:S(2)}) copy-start(f32[4,256,1,2,128]{1,4,3,0,2:T(8,128)} %custom-call.10) | copy-start | bytes 3145732
  325.0 2.7 copy-start.19
  325.6 2.2 copy-start.36
  325.6 2.2 copy-start.37
  325.6 2.9 copy-start.49
  325.6 71.5 %copy-start.5 = (bf16[128,1024]{1,0:T(8,128)(2,1)S(1)}, bf16[128,1024]{1,0:T(8,128)(2,1)}, u32[]{:S(2)}) copy-start(bf16[128,1024]{1,0:T(8,128)(2,1)} %param.21) | copy-start | bytes 786436
  327.7 106.1 %all-gather.19.cloned.1.call-start = ((), (), s32[]{:S(2)}) async-start(), calls=%async_computation.14 | async-start | bytes 1671168 | tf_op jit(solution)/shard_map/all_gather | solution.py:213
  328.4 160.9 %all-gather.17.cloned.1.call-start = ((), (), s32[]{:S(2)}) async-start(), calls=%async_computation.13 | async-start | bytes 2359296 | tf_op jit(solution)/shard_map/all_gather | solution.py:218
  400.0 143.5 %all-gather.21.cloned.1.call-start = ((), (), s32[]{:S(2)}) async-start(), calls=%async_computation.15 | async-start | bytes 2359296 | tf_op jit(solution)/shard_map/all_gather | solution.py:231
  400.7 235.4 %all-gather.23.cloned.1.call-start = ((), (), s32[]{:S(2)}) async-start(), calls=%async_computation.16 | async-start | bytes 2359296 | tf_op jit(solution)/shard_map/all_gather | solution.py:243
  424.8 118.8 %copy-start.24 = (bf16[384,1024]{0,1:T(8,128)(2,1)}, bf16[384,1024]{0,1:T(8,128)(2,1)S(1)}, u32[]{:S(2)}) copy-start(bf16[384,1024]{0,1:T(8,128)(2,1)S(1)} %all_gather.53) | copy-start | bytes 2359300
  543.5 5.2 copy-start.55
  548.7 1.9 copy-start.58
  548.7 1.9 copy-start.60
  581.7 1.8 copy-start.35
  581.7 1.8 copy-start.33
  582.5 56.8 %copy-start.47 = (f32[128]{0:T(128)}, f32[128]{0:T(128)S(1)}, u32[]{:S(2)}) copy-start(f32[128]{0:T(128)S(1)} %multiply_multiply_fusion.4) | copy-start | bytes 1540
  583.4 313.1 %reduce-scatter.14.cloned.1.call-start = ((), (), s32[]{:S(2)}) async-start(), calls=%async_computation.18 | async-start | bytes 4456448 | tf_op jit(solution)/shard_map/reduce_scatter | solution.py:295
  646.1 2.6 copy-start.26
  646.1 2.6 copy-start.56
  825.5 137.0 %reduce-scatter.12.cloned.1.call-start = ((), (), s32[]{:S(2)}) async-start(), calls=%async_computation.17 | async-start | bytes 4456448 | tf_op jit(solution)/shard_map/reduce_scatter | solution.py:292
  826.2 205.6 %reduce-scatter.18.cloned.1.call-start = ((), (), s32[]{:S(2)}) async-start(), calls=%async_computation.20 | async-start | bytes 2506752
  826.7 2.8 copy-start.54
  826.7 2.8 copy-start.59
  826.7 2.8 copy-start.61
  841.1 135.5 %all-to-all-start = ((bf16[8,128,1024]{2,1,0:T(8,128)(2,1)}), bf16[8,128,1024]{2,1,0:T(8,128)(2,1)}, u32[]{:S(2)}, u32[]{:S(2)}) async-start(bf16[8,128,1024]{2,1,0:T(8,128)(2,1)} %bitcast.391), calls=%async_computation.1 | async-start | bytes 4194304 | tf_op jit(solution)/shard_map/all_to_all | solution.py:23
  845.5 267.7 %reduce-scatter.16.cloned.1.call-start = ((), (), s32[]{:S(2)}) async-start(), calls=%async_computation.19 | async-start | bytes 1671168
  848.5 1.8 copy-start.4
  848.5 2.0 copy-start.7
  848.5 2.2 copy-start.18
  848.5 2.2 copy-start.44
  851.1 2.0 copy-start.53
  854.6 110.9 %copy-start.15 = (f32[1024,1,64]{0,2,1:T(8,128)S(1)}, f32[1024,1,64]{0,2,1:T(8,128)}, u32[]{:S(2)}) copy-start(f32[1024,1,64]{0,2,1:T(8,128)} %get-tuple-element.686) | copy-start | bytes 786436
  897.6 69.8 %copy-start.42 = (f32[128]{0:T(128)S(1)}, f32[128]{0:T(128)}, u32[]{:S(2)}) copy-start(f32[128]{0:T(128)} %copy-done.41) | copy-start | bytes 1540
  965.6 3.8 copy-start.39
  967.4 2.2 copy-start.27
  967.4 2.2 copy-start.52
  976.6 62.3 %all-to-all-start.2 = ((bf16[8,128,1024]{2,1,0:T(8,128)(2,1)}), bf16[8,128,1024]{2,1,0:T(8,128)(2,1)S(1)}, u32[]{:S(2)}, u32[]{:S(2)}) async-start(bf16[8,128,1024]{2,1,0:T(8,128)(2,1)} %bitcast.392), calls=%async_computation.5 | async-start | bytes 4194304 | tf_op jit(solution)/shard_map/all_to_all | solution.py:23
  1033.9 6.1 copy-start.31
  1033.9 6.1 copy-start.46
  1035.4 75.4 %copy-start.51 = (f32[128]{0:T(128)S(1)}, f32[128]{0:T(128)}, u32[]{:S(2)}) copy-start(f32[128]{0:T(128)} %copy-done.50) | copy-start | bytes 1540
  1035.4 75.4 %copy-start.9 = (f32[128,1024]{1,0:T(8,128)S(1)}, f32[128,1024]{1,0:T(8,128)}, u32[]{:S(2)}) copy-start(f32[128,1024]{1,0:T(8,128)} %copy-done.8) | copy-start | bytes 1572868
  1035.4 75.4 %copy-start.11 = (bf16[128,1024]{1,0:T(8,128)(2,1)S(1)}, bf16[128,1024]{1,0:T(8,128)(2,1)}, u32[]{:S(2)}) copy-start(bf16[128,1024]{1,0:T(8,128)(2,1)} %reduce-scatter.10.cloned.1.call-done) | copy-start | bytes 786436
  1035.4 75.4 %copy-start.17 = (bf16[128,1024]{1,0:T(8,128)(2,1)S(1)}, bf16[128,1024]{1,0:T(8,128)(2,1)}, u32[]{:S(2)}) copy-start(bf16[128,1024]{1,0:T(8,128)(2,1)} %param.35) | copy-start | bytes 786436
  1035.4 75.4 %copy-start.48 = (f32[128]{0:T(128)S(1)}, f32[128]{0:T(128)}, u32[]{:S(2)}) copy-start(f32[128]{0:T(128)} %copy-done.47) | copy-start | bytes 1540
  1110.8 6.4 copy-start.1
  (13 other events, 14.6 us)
Sparse Core Ops, SparseCore 0:
  10.3 36.2 all-gather.10
  49.5 55.1 all-gather.8
  112.1 36.1 all-gather.14
  213.7 33.4 all-gather.12
  327.8 69.1 reduce-scatter.9
  399.2 34.5 all-gather.18
  436.7 52.6 all-gather.16
  491.7 51.7 all-gather.20
  583.6 52.5 all-gather.22
  825.6 70.8 reduce-scatter.13
  898.9 63.5 reduce-scatter.11
  964.8 67.0 reduce-scatter.17
  1034.2 60.7 reduce-scatter.15
where the time goes:
time: 1140 us; the launch traced here: 1120 us
  waiting for transfers between devices  423 us (37%)
  local copies, waits for them, and re-layouts  248 us (22%)
  blocking collectives  175 us (15%)
  matrix products  135 us (12%)
  other arithmetic  66.5 us (6%)
  loops' own time  47.7 us (4%)
  between operations  16.6 us (1%)
  starting transfers between devices  11.8 us (1%)
    reduce_scatter x1, waiting for transfers between devices, per_device(): lax.psum_scatter(jnp.dot(attn_low, w_proj, preferred_element_type=jnp.flo...  68.5 us
    psum x1, blocking collectives, per_device(): lax.psum((grad_gain_attn, grad_gain_query, grad_gain_key, grad_gain_ffn),...  68.2 us
    reduce_scatter x1, waiting for transfers between devices, per_device(): lax.psum_scatter(key_grad_all.astype(jnp.bfloat16), 'ctx', scatter_dimens...  64.9 us
    all_gather x1, waiting for transfers between devices, per_device(): rows_two = lax.all_gather(normal_two, 'tp', axis=0, tiled=True)  55.6 us
    all_gather x1, waiting for transfers between devices, per_device(): lax.all_gather(grad_resid.astype(jnp.bfloat16), 'tp', axis=0, tiled=True)  52.6 us
    all_gather x1, waiting for transfers between devices, per_device(): grad_rows = lax.all_gather(out_grad, 'tp', axis=0, tiled=True)  48.6 us
    unnamed x15, waiting for transfers between devices  47.5 us
    dynamic_update_slice x8, local copies, waits for them, and re-layouts, grad_step(): lax.dynamic_update_slice_in_dim(key_grad_all, grad_key.reshape(seq_count,...  43.9 us
  transfers between devices with their start and end apart: 15, of which 9 were waited for; matrix products, arithmetic and copies ran while one was open for 18% of the time, Pallas kernels for 0%

commit v1 on v0

v1 whole, which is shorter than its diff:
```python
import functools
import math

import jax
import jax.numpy as jnp
from jax import lax
from jax.experimental import pallas as pl
from jax.experimental.pallas import tpu as pltpu
from jax.sharding import PartitionSpec as P

HD = 128
BLK = 128
EPS = 1e-06
THETA = 1000000.0
SCALE = HD ** (-0.5)
LOG2E = math.log2(math.e)
LN2 = math.log(2.0)
BF = jnp.bfloat16
F32 = jnp.float32
ALL = ("ctx", "tp")
RING = (0, 1, 3, 2)
ROWS = 1024
KEYS = 4096
FWD_KEYS = 512
BWD_KEYS = 512
VMEM = pltpu.CompilerParams(vmem_limit_bytes=48 * 1024 * 1024)


def cost(us):
    return pl.CostEstimate(flops=int(us * 1e9), bytes_accessed=int(us * 1e6), transcendentals=0)


def place_of(x, y, z, core):
    x, y, z, core = x % 4, y % 4, z % 4, core % 2
    return (((x % 2) * 4 + z) * 2 + core) * 8 + y * 2 + x // 2


def all_places():
    return [(x, y, z, c) for x in range(4) for y in range(4) for z in range(4) for c in range(2)]


def shift(value, dx=0, dy=0, dz=0, dcore=0):
    pairs = [
        (place_of(x, y, z, c), place_of(x + dx, y + dy, z + dz, c + dcore)) for x, y, z, c in all_places()
    ]
    return lax.ppermute(value, ALL, pairs)


def weight_pairs(step):
    pairs = []
    for x, y, z, c in all_places():
        pairs.append(
            (place_of(x, y, z, c), place_of((x // 2) * 2 + y // 2, (2 * (x % 2) + c + step) % 4, z, y % 2))
        )
    return pairs


def contract_last(left_side, right_side):
    return lax.dot_general(left_side, right_side, (((1,), (1,)), ((), ())), preferred_element_type=F32)


def contract_first(left_side, right_side):
    return lax.dot_general(left_side, right_side, (((0,), (0,)), ((), ())), preferred_element_type=F32)


def dot(left_side, right_side):
    return jnp.dot(left_side, right_side, preferred_element_type=F32)


def gather_rows(own):
    half = jnp.concatenate([own] + [shift(own, dx=-d) for d in RING[1:]], axis=0)
    return jnp.concatenate([half, shift(half, dcore=1)], axis=0)


def reduce_rows(partial_low):
    half = partial_low.shape[0] // 2
    got = shift(partial_low[half:], dcore=1)
    both = (partial_low[:half].astype(F32) + got.astype(F32)).astype(BF)
    rows = half // 4
    total = both[:rows].astype(F32)
    arrived = [shift(both[k * rows : (k + 1) * rows], dx=RING[k]) for k in range(1, 4)]
    for part in arrived:
        total = total + part.astype(F32)
    return total


def after(values, *others):
    return lax.optimization_barrier((values, others))[0]


def assemble_kernel(widths, offs_ref, *refs):
    slots, outs = refs[:4], refs[4:]
    for s in range(4):
        for k in range(4):
            rows = pl.ds(pl.multiple_of(offs_ref[s * 4 + k], 64), 64)
            col = 0
            for out, width in zip(outs, widths, strict=True):
                out[rows, :] = slots[s][k * 64 : (k + 1) * 64, col : col + width]
                col += width


def to_users(shard):
    return jnp.concatenate([lax.ppermute(shard, ALL, weight_pairs(step)) for step in range(4)], axis=0)


def along_z(mine):
    return [mine] + [shift(mine, dz=-d) for d in RING[1:]]


def assembled(slots, widths, offs):
    vmem = pl.BlockSpec(memory_space=pltpu.VMEM)
    return pl.pallas_call(
        functools.partial(assemble_kernel, widths),
        out_shape=[jax.ShapeDtypeStruct((ROWS, w), BF) for w in widths],
        in_specs=[pl.BlockSpec(memory_space=pltpu.SMEM)] + [vmem] * 4,
        out_specs=[vmem] * len(widths),
        compiler_params=VMEM,
        cost_estimate=cost(1 + sum(widths) / 512),
        name="assemble",
    )(offs, *slots)


def sum_ring(value, axis):
    arrived = [shift(value, **{axis: d}) for d in RING[1:]]
    return value + arrived[0] + (arrived[1] + arrived[2])


def reduce_along_z(grads, z):
    width = grads.shape[1]
    parts = grads.astype(BF).reshape(2, 4, 2, 64, width)

    def rows_for(d):
        return lax.dynamic_index_in_dim(parts, (z + d) % 4, 1, keepdims=False)

    total = rows_for(0).astype(F32)
    arrived = [shift(rows_for(d), dz=d) for d in RING[1:]]
    for part in arrived:
        total = total + part.astype(F32)
    return total.astype(BF).reshape(4, 64, width)


def to_owners(low, y):
    result = None
    for step in range(4):
        piece = lax.dynamic_index_in_dim(low, (y - step) % 4, 0, keepdims=False)
        back = [(b, a) for a, b in weight_pairs(step)]
        got = lax.ppermute(piece, ALL, back).astype(F32)
        result = got if result is None else result + got
    return result


def head_norm(pre):
    return pre * lax.rsqrt(jnp.mean(pre * pre, axis=-1, keepdims=True) + EPS)


def qkv_kernel(tok_ref, gain_ref, w_ref, qg_ref, kg_ref, cos_ref, sin_ref, norm_ref, q_ref, kv_ref, pre_ref):
    tok = tok_ref[...].astype(F32)
    rate = lax.rsqrt(jnp.mean(tok * tok, axis=-1, keepdims=True) + EPS)
    low = (tok * rate * gain_ref[...]).astype(BF)
    norm_ref[...] = low
    proj = dot(low, w_ref[...])
    cos, sin = cos_ref[...], sin_ref[...]
    pre_ref[...] = proj[:, : 3 * HD]
    for h in range(3):
        gain = qg_ref[...] if h < 2 else kg_ref[...]
        u = head_norm(proj[:, h * HD : (h + 1) * HD]) * gain
        u = u * cos + pltpu.roll(u, HD // 2, 1) * sin
        if h < 2:
            q_ref[:, h * HD : (h + 1) * HD] = (u * (SCALE * LOG2E)).astype(BF)
        else:
            kv_ref[:, :HD] = u.astype(BF)
    kv_ref[:, HD:] = proj[:, 3 * HD :].astype(BF)


def project(tokens, gain, w_qkv, q_gain, k_gain, cos, sin):
    rows, d = tokens.shape
    step = 256
    by_rows = lambda w: pl.BlockSpec((step, w), lambda i: (i, 0))
    whole = lambda a: pl.BlockSpec(a.shape, lambda i: (0, 0))
    return pl.pallas_call(
        qkv_kernel,
        grid=(rows // step,),
        in_specs=[by_rows(d), whole(gain), whole(w_qkv), whole(q_gain), whole(k_gain), by_rows(HD), by_rows(HD)],
        out_specs=[by_rows(d), by_rows(2 * HD), by_rows(2 * HD), by_rows(3 * HD)],
        out_shape=[
            jax.ShapeDtypeStruct((rows, d), BF),
            jax.ShapeDtypeStruct((rows, 2 * HD), BF),
            jax.ShapeDtypeStruct((rows, 2 * HD), BF),
            jax.ShapeDtypeStruct((rows, 3 * HD), F32),
        ],
        compiler_params=VMEM,
        cost_estimate=cost(5),
        name="project",
    )(tokens, gain, w_qkv, q_gain, k_gain, cos, sin)


def qkv_back_kernel(
    dq_ref, kv0, kv1, kv2, kv3, pre_ref, cos_ref, sin_ref, qg_ref, kg_ref, tok_ref, w_ref,
    gqkv_ref, gnorm_ref, gattn_ref, gq_ref, gk_ref,
):
    @pl.when(pl.program_id(0) == 0)
    def _():
        gattn_ref[...] = jnp.zeros_like(gattn_ref)
        gq_ref[...] = jnp.zeros_like(gq_ref)
        gk_ref[...] = jnp.zeros_like(gk_ref)

    dkv = kv0[...].astype(F32) + kv1[...].astype(F32) + kv2[...].astype(F32) + kv3[...].astype(F32)
    cos, sin = cos_ref[...], sin_ref[...]
    for h in range(3):
        grad = dq_ref[:, h * HD : (h + 1) * HD] if h < 2 else dkv[:, :HD]
        gain = qg_ref[...] if h < 2 else kg_ref[...]
        u = pre_ref[:, h * HD : (h + 1) * HD]
        rate = lax.rsqrt(jnp.mean(u * u, axis=-1, keepdims=True) + EPS)
        n = u * rate
        g = grad * cos - pltpu.roll(grad, HD // 2, 1) * sin
        gained = gain * g
        pre_grad = (gained - n * jnp.mean(gained * n, axis=-1, keepdims=True)) * rate
        gqkv_ref[:, h * HD : (h + 1) * HD] = pre_grad.astype(BF)
        sums = jnp.sum((g * n).reshape(-1, 8, HD), axis=0)
        if h < 2:
            gq_ref[...] += sums
        else:
            gk_ref[...] += sums
    gqkv_ref[:, 3 * HD :] = dkv[:, HD:].astype(BF)
    gnorm = contract_last(gqkv_ref[...], w_ref[...])
    gnorm_ref[...] = gnorm.astype(BF)
    tok = tok_ref[...].astype(F32)
    xhat = tok * lax.rsqrt(jnp.mean(tok * tok, axis=-1, keepdims=True) + EPS)
    gattn_ref[...] += jnp.sum((gnorm * xhat).reshape(-1, 8, gnorm.shape[1]), axis=0)


def project_back(dq, dkv, pre, cos, sin, q_gain, k_gain, tokens, w_qkv):
    rows, d = tokens.shape
    step = 256
    by_rows = lambda w: pl.BlockSpec((step, w), lambda i: (i, 0))
    whole = lambda a: pl.BlockSpec(a.shape, lambda i: (0, 0))
    fixed = lambda w: pl.BlockSpec((8, w), lambda i: (0, 0))
    return pl.pallas_call(
        qkv_back_kernel,
        grid=(rows // step,),
        in_specs=[by_rows(2 * HD)]
        + [by_rows(2 * HD)] * 4
        + [by_rows(3 * HD), by_rows(HD), by_rows(HD), whole(q_gain), whole(k_gain), by_rows(d), whole(w_qkv)],
        out_specs=[by_rows(4 * HD), by_rows(d), fixed(d), fixed(HD), fixed(HD)],
        out_shape=[
            jax.ShapeDtypeStruct((rows, 4 * HD), BF),
            jax.ShapeDtypeStruct((rows, d), BF),
            jax.ShapeDtypeStruct((8, d), F32),
            jax.ShapeDtypeStruct((8, HD), F32),
            jax.ShapeDtypeStruct((8, HD), F32),
        ],
        compiler_params=VMEM,
        cost_estimate=cost(9),
        name="project_back",
    )(dq, *dkv, pre, cos, sin, q_gain, k_gain, tokens, w_qkv)


def stacked(ref, i):
    rows = ref[pl.ds(pl.multiple_of(i * BLK, BLK), BLK), :]
    return jnp.concatenate([rows[:, :HD], rows[:, HD:]], axis=0)


def allowed_keys(start, place, first, count):
    pos = first + lax.broadcasted_iota(jnp.int32, (count, 2 * BLK), 0)
    return (pos >= start) & (pos <= place)


def query_places(qblk):
    lane = lax.broadcasted_iota(jnp.int32, (1, 2 * BLK), 1)
    return qblk * BLK + (lane & (BLK - 1))


def attend_kernel(kblk, qblk, low, start_ref, q_ref, kv0, kv1, kv2, kv3, out_ref, o_ref, lse_ref, keys, values_t):
    for s, ref in enumerate((kv0, kv1, kv2, kv3)):
        for j in range(8):
            at = pl.multiple_of(kblk[s * 8 + j] * BLK, BLK)
            keys[pl.ds(at, BLK), :] = ref[j * BLK : (j + 1) * BLK, :HD]
            values_t[:, pl.ds(at, BLK)] = ref[j * BLK : (j + 1) * BLK, HD:].T
    chunk = FWD_KEYS // BLK

    def one_block(i, _):
        q = stacked(q_ref, i)
        start = start_ref[i]
        place = query_places(qblk[i])

        def one_chunk(c, carry):
            acc, total = carry
            first = pl.multiple_of(c * FWD_KEYS, FWD_KEYS)
            scores = contract_last(keys[pl.ds(first, FWD_KEYS), :], q)
            ok = allowed_keys(start, place, first, FWD_KEYS)
            weights = jnp.where(ok, jnp.exp2(scores), 0.0)
            total = total + jnp.sum(weights.reshape(-1, 8, 2 * BLK), axis=0)
            acc = acc + dot(values_t[:, pl.ds(first, FWD_KEYS)], weights.astype(BF))
            return acc, total

        acc, total = lax.fori_loop(
            low[i] // chunk,
            qblk[i] // chunk + 1,
            one_chunk,
            (jnp.zeros((HD, 2 * BLK), F32), jnp.zeros((8, 2 * BLK), F32)),
        )
        total = jnp.sum(total, axis=0, keepdims=True)
        o = acc * (1.0 / total)
        o_ref[i] = o
        lse_ref[i] = jnp.log2(total)
        rows = o.T.astype(BF)
        out_ref[pl.ds(pl.multiple_of(i * BLK, BLK), BLK), :] = jnp.concatenate([rows[:BLK], rows[BLK:]], axis=1)
        return 0

    lax.fori_loop(0, ROWS // BLK, one_block, 0)


def attend(kblk, qblk, low, start, q, kv):
    smem = pl.BlockSpec(memory_space=pltpu.SMEM)
    vmem = pl.BlockSpec(memory_space=pltpu.VMEM)
    blocks = ROWS // BLK
    return pl.pallas_call(
        attend_kernel,
        in_specs=[smem] * 3 + [vmem] * 6,
        out_specs=[vmem] * 3,
        out_shape=[
            jax.ShapeDtypeStruct((ROWS, 2 * HD), BF),
            jax.ShapeDtypeStruct((blocks, HD, 2 * BLK), F32),
            jax.ShapeDtypeStruct((blocks, 1, 2 * BLK), F32),
        ],
        scratch_shapes=[pltpu.VMEM((KEYS, HD), BF), pltpu.VMEM((HD, KEYS), BF)],
        compiler_params=VMEM,
        cost_estimate=cost(14),
        name="attend",
    )(kblk, qblk, low, start, q, *kv)


def attend_back_kernel(
    kblk, qblk, low, start_ref, q_ref, do_ref, o_ref, lse_ref, kv0, kv1, kv2, kv3,
    dq_ref, dkv0, dkv1, dkv2, dkv3, keys, keys_t, values, dk, dv,
):
    for s, ref in enumerate((kv0, kv1, kv2, kv3)):
        for j in range(8):
            at = pl.multiple_of(kblk[s * 8 + j] * BLK, BLK)
            key = ref[j * BLK : (j + 1) * BLK, :HD]
            keys[pl.ds(at, BLK), :] = key
            keys_t[:, pl.ds(at, BLK)] = key.T
            values[pl.ds(at, BLK), :] = ref[j * BLK : (j + 1) * BLK, HD:]
    dk[...] = jnp.zeros_like(dk)
    dv[...] = jnp.zeros_like(dv)
    chunk = BWD_KEYS // BLK

    def one_block(i, _):
        q = stacked(q_ref, i)
        do = stacked(do_ref, i)
        delta = jnp.sum(do.astype(F32).T * o_ref[i], axis=0, keepdims=True)
        lse = lse_ref[i]
        start = start_ref[i]
        place = query_places(qblk[i])

        def one_chunk(c, acc):
            first = pl.multiple_of(c * BWD_KEYS, BWD_KEYS)
            here = pl.ds(first, BWD_KEYS)
            scores = contract_last(keys[here, :], q)
            ok = allowed_keys(start, place, first, BWD_KEYS)
            probs = jnp.where(ok, jnp.exp2(scores - lse), 0.0)
            dprobs = contract_last(values[here, :], do)
            dscores = (probs * (dprobs - delta)).astype(BF)
            dv[here, :] += dot(probs.astype(BF), do)
            dk[here, :] += dot(dscores, q)
            return acc + dot(keys_t[:, here], dscores)

        acc = lax.fori_loop(low[i] // chunk, qblk[i] // chunk + 1, one_chunk, jnp.zeros((HD, 2 * BLK), F32))
        rows = acc.T * SCALE
        dq_ref[pl.ds(pl.multiple_of(i * BLK, BLK), BLK), :] = jnp.concatenate([rows[:BLK], rows[BLK:]], axis=1)
        return 0

    lax.fori_loop(0, ROWS // BLK, one_block, 0)
    for s, ref in enumerate((dkv0, dkv1, dkv2, dkv3)):
        for j in range(8):
            at = pl.multiple_of(kblk[s * 8 + j] * BLK, BLK)
            ref[j * BLK : (j + 1) * BLK, :HD] = (dk[pl.ds(at, BLK), :] * LN2).astype(BF)
            ref[j * BLK : (j + 1) * BLK, HD:] = dv[pl.ds(at, BLK), :].astype(BF)


def attend_back(kblk, qblk, low, start, q, do, o, lse, kv):
    smem = pl.BlockSpec(memory_space=pltpu.SMEM)
    vmem = pl.BlockSpec(memory_space=pltpu.VMEM)
    return pl.pallas_call(
        attend_back_kernel,
        in_specs=[smem] * 3 + [vmem] * 9,
        out_specs=[vmem] * 5,
        out_shape=[jax.ShapeDtypeStruct((ROWS, 2 * HD), F32)] + [jax.ShapeDtypeStruct((ROWS, 2 * HD), BF)] * 4,
        scratch_shapes=[
            pltpu.VMEM((KEYS, HD), BF),
            pltpu.VMEM((HD, KEYS), BF),
            pltpu.VMEM((KEYS, HD), BF),
            pltpu.VMEM((KEYS, HD), F32),
            pltpu.VMEM((KEYS, HD), F32),
        ],
        compiler_params=VMEM,
        cost_estimate=cost(20),
        name="attend_back",
    )(kblk, qblk, low, start, q, do, o, lse, *kv)


def per_device(
    tokens,
    block_table,
    doc_ids,
    attn_gain,
    w_query,
    w_key,
    w_value,
    query_gain,
    key_gain,
    w_out,
    ffn_gain,
    w_gate,
    w_up,
    w_down,
    out_grad,
):
    ctx_rank = lax.axis_index("ctx")
    tp_rank = lax.axis_index("tp")
    x_lo, z, core = ctx_rank // 8, (ctx_rank // 2) % 4, ctx_rank % 2
    y, x_hi = tp_rank // 2, tp_rank % 2
    x = 2 * x_hi + x_lo
    d_model = tokens.shape[1]
    q_width, k_width, ff_local = w_query.shape[1], w_key.shape[1], w_gate.shape[1]

    ring = jnp.array(RING, jnp.int32)
    xs = ((x + ring) % 4)[None, None, :]
    zs = ((z + ring) % 4)[:, None, None]
    cores = ((core + jnp.arange(2, dtype=jnp.int32)) % 2)[None, :, None]
    entry = ((((xs % 2) * 4 + zs) * 2 + cores) * 2 + xs // 2).reshape(32)
    table = block_table.reshape(32)
    kblk = jnp.sum(
        jnp.where(entry[:, None] == jnp.arange(32, dtype=jnp.int32)[None, :], table[None, :], 0), axis=1
    ).astype(jnp.int32)
    qblk = kblk[:8]
    docs = lax.dynamic_index_in_dim(doc_ids, y, 0, keepdims=False)
    firsts = jnp.sum((docs[None, :] < jnp.arange(4, dtype=jnp.int32)[:, None]).astype(jnp.int32), axis=1)
    place = qblk[:, None] * BLK + jnp.arange(BLK, dtype=jnp.int32)[None, :]
    start = jnp.max(
        jnp.where(firsts[:, None, None] <= place[None], firsts[:, None, None], 0), axis=0
    )
    low = start[:, 0] // BLK
    start2 = jnp.concatenate([start, start], axis=1)[:, None, :]
    pos = (place - start).reshape(ROWS)
    freq = jnp.power(jnp.float32(THETA), -(jnp.arange(HD // 2, dtype=F32) * (2.0 / HD)))
    angles = pos.astype(F32)[:, None] * freq[None, :]
    cos_half, sin_half = jnp.cos(angles), jnp.sin(angles)
    cos = jnp.concatenate([cos_half, cos_half], axis=1)
    sin = jnp.concatenate([-sin_half, sin_half], axis=1)
    bits = ((y - jnp.arange(4, dtype=jnp.int32)) % 4)[None, :]
    offs = (((bits // 2) * 4 + zs.reshape(4, 1)) * 2 + bits % 2).reshape(16) * 64

    def head_gain(gain):
        return jnp.concatenate([gain, jnp.zeros((64 - gain.shape[0],), BF)])

    gains = jnp.stack([attn_gain, ffn_gain, head_gain(query_gain), head_gain(key_gain)], axis=1)
    gains = jnp.concatenate([gains, jnp.zeros((64, 124), BF)], axis=1)
    w_o, w_d = w_out.shape[0], w_down.shape[0]
    first_mine = to_users(jnp.concatenate([w_query, w_key, w_value, gains], axis=1))
    w_qkv, gain_cols = assembled(along_z(first_mine), (q_width + 2 * k_width, 128), offs)
    second_shard = jnp.concatenate([w_out.T, w_gate, w_up, w_down.T], axis=1)
    second_mine = to_users(after(second_shard, first_mine))
    gain_rows = gain_cols[:, :8].astype(F32).T
    gain_attn, gain_ffn = gain_rows[0:1], gain_rows[1:2]
    gain_query = gain_rows[2].reshape(16, 64)[:, :8].reshape(1, HD)
    gain_key = gain_rows[3].reshape(16, 64)[:, :8].reshape(1, HD)

    rows_tok = gather_rows(tokens)
    rows_tok = after(rows_tok, second_mine)
    normal_one, q, kv, pre = project(rows_tok, gain_attn, w_qkv, gain_query, gain_key, cos, sin)
    kv_all = along_z(kv)
    grad_rows = gather_rows(after(out_grad, kv))
    out_mine, ffn_mine = after((second_mine[:, :w_o], second_mine[:, w_o:]), *kv_all)
    out_slots = along_z(out_mine)
    attn_low, o, lse = attend(kblk, qblk, low, start2, q, kv_all)
    (w_proj,) = assembled(out_slots, (w_o,), offs)
    w_gu, w_dn = assembled(along_z(after(ffn_mine, *out_slots)), (2 * ff_local, w_d), offs)
    grad_rows = after(grad_rows, attn_low)
    resid = tokens.astype(F32) + reduce_rows(contract_last(attn_low, w_proj).astype(BF))
    rate_two = lax.rsqrt(jnp.mean(resid * resid, axis=-1, keepdims=True) + EPS)
    xhat_two = resid * rate_two
    rows_two = gather_rows((xhat_two * gain_ffn).astype(BF))
    gate_up = dot(rows_two, w_gu)
    gate, up_proj = gate_up[:, :ff_local], gate_up[:, ff_local:]
    sigmoid_gate = jax.nn.sigmoid(gate)
    silu_gate = gate * sigmoid_gate
    hidden = (silu_gate * up_proj).astype(BF)
    grad_hidden = dot(grad_rows, w_dn)
    grad_gate = grad_hidden * up_proj * (sigmoid_gate * (1.0 + gate * (1.0 - sigmoid_gate)))
    grad_up = grad_hidden * silu_gate
    grad_gu = jnp.concatenate([grad_gate, grad_up], axis=1).astype(BF)
    grad_norm_two = reduce_rows(contract_last(grad_gu, w_gu).astype(BF))
    ffn_low = reduce_along_z(
        jnp.concatenate([contract_first(rows_two, grad_gu), contract_first(grad_rows, hidden)], axis=1), z
    )
    grad_gain_ffn = jnp.sum(grad_norm_two * xhat_two, axis=0)
    gained = grad_norm_two * gain_ffn
    grad_resid = out_grad.astype(F32) + (
        gained - xhat_two * jnp.mean(gained * xhat_two, axis=-1, keepdims=True)
    ) * rate_two
    branch_rows = gather_rows(grad_resid.astype(BF))
    grad_attn = dot(branch_rows, w_proj).astype(BF)
    grad_attn, ffn_low = lax.optimization_barrier((grad_attn, ffn_low))
    out_low = reduce_along_z(contract_first(branch_rows, attn_low), z)
    out = (resid + reduce_rows(after(contract_last(hidden, w_dn).astype(BF), branch_rows))).astype(BF)

    dq, *dkv = attend_back(kblk, qblk, low, start2, q, grad_attn, o, lse, kv_all)
    dkv_all = [dkv[0]] + [shift(dkv[k], dz=RING[k]) for k in range(1, 4)]
    late_owned = to_owners(jnp.concatenate([out_low, ffn_low], axis=2), y)
    dq, out, late_owned = lax.optimization_barrier((dq, out, late_owned))
    grad_qkv, grad_one, sum_attn, sum_query, sum_key = project_back(
        dq, dkv_all, pre, cos, sin, gain_query, gain_key, rows_tok, w_qkv
    )
    grad_norm_one = reduce_rows(grad_one)
    tok = tokens.astype(F32)
    rate_one = lax.rsqrt(jnp.mean(tok * tok, axis=-1, keepdims=True) + EPS)
    xhat_one = tok * rate_one
    gained = grad_norm_one * gain_attn
    grad_x = (
        grad_resid + (gained - xhat_one * jnp.mean(gained * xhat_one, axis=-1, keepdims=True)) * rate_one
    ).astype(BF)
    qkv_owned = to_owners(reduce_along_z(contract_first(normal_one, grad_qkv), z), y)
    sums = jnp.concatenate(
        [jnp.sum(sum_attn, axis=0), grad_gain_ffn, jnp.sum(sum_query, axis=0), jnp.sum(sum_key, axis=0)]
    )
    sums = sums + shift(sums, dcore=1)
    for axis in ("dx", "dz", "dy"):
        sums = sum_ring(sums, axis)
    share = d_model // 16

    def own_part(first, size):
        return lax.dynamic_slice_in_dim(sums, first + ctx_rank * size, size)

    return (
        out,
        grad_x,
        own_part(0, share),
        qkv_owned[:, :q_width],
        qkv_owned[:, q_width : q_width + k_width],
        qkv_owned[:, q_width + k_width :],
        own_part(2 * d_model, HD // 16),
        own_part(2 * d_model + HD, HD // 16),
        late_owned[:, :w_o].T,
        own_part(d_model, share),
        late_owned[:, w_o : w_o + ff_local],
        late_owned[:, w_o + ff_local : w_o + 2 * ff_local],
        late_owned[:, w_o + 2 * ff_local :].T,
    )


def solution(mesh):
    in_specs = (
        P(("ctx", "tp"), None),
        P(),
        P(),
        P("ctx"),
        P("ctx", "tp"),
        P("ctx", "tp"),
        P("ctx", "tp"),
        P("ctx"),
        P("ctx"),
        P("tp", "ctx"),
        P("ctx"),
        P("ctx", "tp"),
        P("ctx", "tp"),
        P("tp", "ctx"),
        P(("ctx", "tp"), None),
    )
    out_specs = (
        P(("ctx", "tp"), None),
        P(("ctx", "tp"), None),
        P("ctx"),
        P("ctx", "tp"),
        P("ctx", "tp"),
        P("ctx", "tp"),
        P("ctx"),
        P("ctx"),
        P("tp", "ctx"),
        P("ctx"),
        P("ctx", "tp"),
        P("ctx", "tp"),
        P("tp", "ctx"),
    )
    return jax.shard_map(
        per_device, mesh=mesh, in_specs=in_specs, out_specs=out_specs, check_vma=False
    )
```

time: 1140 us -> 405 us (0.36)
  waiting for transfers between devices: 423 us -> 161 us
  local copies, waits for them, and re-layouts: 248 us -> 29.8 us
  blocking collectives: 175 us -> 0 us
  matrix products: 135 us -> 16.4 us
  starting transfers between devices: 11.8 us -> 125 us
  other arithmetic: 66.5 us -> 14.6 us
  Pallas kernels: 0 us -> 49.4 us
  loops' own time: 47.7 us -> 0 us
  between operations: 16.6 us -> 2.27 us
    all_gather x8 -> x0, waiting for transfers between devices: 200 us -> none  [the longest x1 55.6 us: per_device(): rows_two = lax.all_gather(normal_two, 'tp', axis=0, tiled=True)]
    reduce_scatter x3 -> x0, waiting for transfers between devices: 175 us -> none  [the longest x1 68.5 us: per_device(): lax.psum_scatter(jnp.dot(attn_low, w_proj, preferred_element_type=jnp.flo...]
    ppermute x0 -> x82, waiting for transfers between devices: none -> 161 us  [the longest x66 157 us: shift(): return lax.ppermute(value, ALL, pairs)]
    ppermute x0 -> x82, starting transfers between devices: none -> 125 us  [the longest x66 80.1 us: shift(): return lax.ppermute(value, ALL, pairs)]
    dot_general x60 -> x3, matrix products: 114 us -> 5.09 us  [dot(): return jnp.dot(left_side, right_side, preferred_element_type=F32)]
    dynamic_update_slice x16 -> x0, local copies, waits for them, and re-layouts: 87.7 us -> none  [the longest x8 43.9 us: grad_step(): lax.dynamic_update_slice_in_dim(key_grad_all, grad_key.reshape(seq_count,...]
    gather x6 -> x0, local copies, waits for them, and re-layouts: 76.8 us -> none  [the longest x1 33.8 us: per_device(): block_table[key_index // pair_rows, key_inner // half_block] * half_block]
    psum x1 -> x0, blocking collectives: 68.2 us -> none  [per_device(): lax.psum((grad_gain_attn, grad_gain_query, grad_gain_key, grad_gain_ffn),...]
  transfers between devices with their start and end apart: 15 -> 82, of which waited for: 9 -> 33; matrix products, arithmetic and copies ran while one was open for 18% -> 8% of each run, Pallas kernels for 0% -> 9%
where the time goes in v1:
time: 405 us; the launch traced here: 398 us
  waiting for transfers between devices  161 us (40%)
  starting transfers between devices  125 us (31%)
  Pallas kernels  49.4 us (12%)
  local copies, waits for them, and re-layouts  29.8 us (7%)
  matrix products  16.4 us (4%)
  other arithmetic  14.6 us (4%)
    ppermute x66, waiting for transfers between devices, shift(): return lax.ppermute(value, ALL, pairs)  157 us
    ppermute x66, starting transfers between devices, shift(): return lax.ppermute(value, ALL, pairs)  80.1 us
    ppermute x8, starting transfers between devices, to_users(): lax.ppermute(shard, ALL, weight_pairs(step))  27.1 us
    pallas_call x1, Pallas kernels, attend_back(): pl.pallas_call(attend_back_kernel, in_specs=[smem] * 3 + [vmem] * 9, out_...  19.3 us
    ppermute x8, starting transfers between devices, to_owners(): got = lax.ppermute(piece, ALL, back).astype(F32)  17.3 us
    unnamed x97, local copies, waits for them, and re-layouts  14.2 us
    pallas_call x1, Pallas kernels, attend(): pl.pallas_call(attend_kernel, in_specs=[smem] * 3 + [vmem] * 6, out_specs...  14.1 us
    pallas_call x1, Pallas kernels, project_back(): pl.pallas_call(qkv_back_kernel, grid=(rows // step,), in_specs=[by_rows(2...  8.57 us
  transfers between devices with their start and end apart: 82, of which 33 were waited for; matrix products, arithmetic and copies ran while one was open for 8% of the time, Pallas kernels for 9%

profile of v1, /device:TPU:1, one launch (start us, length us, event | category | flops | bytes accessed | tf_op | source)
XLA Modules:
  0.0 398.3 jit_solution(2982809089934646886)
XLA Ops:
  6.8 3.6 collective-permute-start.6
  11.9 1.9 collective-permute-start.4
  13.8 2.5 collective-permute-start.2
  18.8 1.9 fusion.34
  27.3 4.5 %collective-permute-start.8 = (bf16[64,1408]{1,0:T(8,128)(2,1)}, bf16[64,1408]{1,0:T(8,128)(2,1)}, u32[]{:S(2)}, u32[]{:S(2)}) collective-permute-start(bf16[64,1408]{1,0:T(8,128)(2,1)} %pad_maximum_fusion.9), channel_id=1, source_target_pairs={{0,0},{8,2},{16,16},{24,18},{32,32},{40,34},{48,48},{56,50},{2,8},... | collective-permute-start | bytes 540680 | tf_op jit(solution)/shard_map/ppermute | solution.py:103
  32.9 2.4 collective-permute-done.8
  35.3 9.3 %collective-permute-start.9 = (bf16[64,1408]{1,0:T(8,128)(2,1)}, bf16[64,1408]{1,0:T(8,128)(2,1)S(1)}, u32[]{:S(2)}, u32[]{:S(2)}) collective-permute-start(bf16[64,1408]{1,0:T(8,128)(2,1)} %pad_maximum_fusion.9), channel_id=1, source_target_pairs={{0,2},{8,4},{16,18},{24,20},{32,34},{40,36},{48,50},{56,52},{2,10}... | collective-permute-start | bytes 540680 | tf_op jit(solution)/shard_map/ppermute | solution.py:103
  45.5 1.8 collective-permute-done.9
  47.3 4.8 %collective-permute-start.10 = (bf16[64,1408]{1,0:T(8,128)(2,1)}, bf16[64,1408]{1,0:T(8,128)(2,1)S(1)}, u32[]{:S(2)}, u32[]{:S(2)}) collective-permute-start(bf16[64,1408]{1,0:T(8,128)(2,1)} %pad_maximum_fusion.9), channel_id=1, source_target_pairs={{0,4},{8,6},{16,20},{24,22},{32,36},{40,38},{48,52},{56,54},{2,12}... | collective-permute-start | bytes 540680 | tf_op jit(solution)/shard_map/ppermute | solution.py:103
  52.2 3.7 collective-permute-start.14
  57.3 1.9 collective-permute-start.12
  63.8 7.0 %collective-permute-done.13.refs_2_ = bf16[256,640]{1,0:T(8,128)(2,1)S(1)} collective-permute-done((bf16[256,640]{1,0:T(8,128)(2,1)S(1)}, bf16[256,640]{1,0:T(8,128)(2,1)S(1)}, u32[]{:S(2)}, u32[]{:S(2)}) %collective-permute-start.13) | collective-permute-done | bytes 327712 | tf_op jit(solution)/shard_map/ppermute | solution.py:46
  72.9 2.3 constant_dynamic-update-slice_fusion.tok_ref
  76.4 5.5 %project.1 = (bf16[1024,1024]{1,0:T(8,128)(2,1)}, bf16[1024,256]{1,0:T(8,128)(2,1)S(1)}, bf16[1024,256]{1,0:T(8,128)(2,1)S(1)}, f32[1024,384]{1,0:T(8,128)S(1)}) custom-call(bf16[1024,1024]{1,0:T(8,128)(2,1)} %constant_dynamic-update-slice_fusion.tok_ref, f32[1,1024]{1,0:T(1,128)S(1)} %get-tuple-element.133.gain_ref, bf16[1024,512]{1,0:T(8,128)(2,1)S(1)} %copy-done.9, ...), custom_call_target="tpu_custom_call" | custom-call | flops 5000000000 | bytes 5000000 | tf_op jit(solution)/shard_map/project/pallas_call | solution.py:180
  83.2 2.3 collective-permute-start.21
  86.2 2.0 collective-permute-start.19
  88.4 9.5 %collective-permute-done.21.kv3 = bf16[1024,256]{1,0:T(8,128)(2,1)S(1)} collective-permute-done((bf16[1024,256]{1,0:T(8,128)(2,1)S(1)}, bf16[1024,256]{1,0:T(8,128)(2,1)S(1)}, u32[]{:S(2)}, u32[]{:S(2)}) %collective-permute-start.21) | collective-permute-done | bytes 524320 | tf_op jit(solution)/shard_map/ppermute | solution.py:46
  97.8 11.9 %collective-permute-done.20.kv2 = bf16[1024,256]{1,0:T(8,128)(2,1)S(1)} collective-permute-done((bf16[1024,256]{1,0:T(8,128)(2,1)S(1)}, bf16[1024,256]{1,0:T(8,128)(2,1)S(1)}, u32[]{:S(2)}, u32[]{:S(2)}) %collective-permute-start.20) | collective-permute-done | bytes 524320 | tf_op jit(solution)/shard_map/ppermute | solution.py:46
  114.3 14.1 %attend.1 = (bf16[1024,256]{1,0:T(8,128)(2,1)S(1)}, f32[8,128,256]{2,1,0:T(8,128)S(1)}, f32[8,1,256]{2,1,0:T(1,128)S(1)}) custom-call(s32[32]{0:T(128)S(1)} %select_reduce_fusion.1.kblk, s32[8]{0:T(128)S(1)} %get-tuple-element.144.qblk, s32[8]{0:T(128)S(1)} %and_select_fusion.3.low, s32[8,1,256]{2,1,0:T(1,128)S(1)} %broadcast_in_dim.32.start_ref, ...), custom_call_target="tpu_custom_call" | custom-call | flops 14000000000 | bytes 14000000 | tf_op jit(solution)/shard_map/attend/pallas_call | solution.py:317
  130.3 1.9 collective-permute-start.28
  132.2 2.3 collective-permute-done.28
  135.1 2.6 collective-permute-start.30
  137.7 2.4 collective-permute-start.17
  140.1 14.9 %collective-permute-done.29 = bf16[128,1024]{1,0:T(8,128)(2,1)S(1)} collective-permute-done((bf16[128,1024]{1,0:T(8,128)(2,1)S(1)}, bf16[128,1024]{1,0:T(8,128)(2,1)S(1)}, u32[]{:S(2)}, u32[]{:S(2)}) %collective-permute-start.29) | collective-permute-done | bytes 262176 | tf_op jit(solution)/shard_map/ppermute | solution.py:46
  157.6 2.4 collective-permute-start.32
  160.0 3.8 collective-permute-done.16
  163.9 3.7 collective-permute-start.18
  168.0 3.8 collective-permute-done.33
  172.1 3.2 collective-permute-start.35
  175.3 8.7 %collective-permute-done.27.refs_3_ = bf16[256,1152]{1,0:T(8,128)(2,1)S(1)} collective-permute-done((bf16[256,1152]{1,0:T(8,128)(2,1)S(1)}, bf16[256,1152]{1,0:T(8,128)(2,1)S(1)}, u32[]{:S(2)}, u32[]{:S(2)}) %collective-permute-start.27) | collective-permute-done | bytes 589856 | tf_op jit(solution)/shard_map/ppermute | solution.py:46
  184.1 13.0 %collective-permute-done.26.refs_2_ = bf16[256,1152]{1,0:T(8,128)(2,1)S(1)} collective-permute-done((bf16[256,1152]{1,0:T(8,128)(2,1)S(1)}, bf16[256,1152]{1,0:T(8,128)(2,1)S(1)}, u32[]{:S(2)}, u32[]{:S(2)}) %collective-permute-start.26) | collective-permute-done | bytes 589856 | tf_op jit(solution)/shard_map/ppermute | solution.py:46
  197.9 2.5 copy-done.31
  200.6 1.9 fusion.51
  202.5 2.5 multiply_convert_fusion.2
  205.0 1.8 convolution_convert_fusion.2
  209.7 4.0 %convolution_convert_fusion.3 = bf16[1024,768]{1,0:T(8,128)(2,1)S(1)} fusion(bf16[1024,1024]{1,0:T(8,128)(2,1)} %copy-done.32, bf16[1024,384]{0,1:T(8,128)(2,1)} %copy-done.37, bf16[1024,384]{0,1:T(8,128)(2,1)} %copy-done.36), kind=kOutput, calls=%fused_computation.15 | convolution fusion | flops 1614544896 | bytes 5242880 | tf_op jit(solution)/shard_map/dot_general | solution.py:63
  213.8 1.8 add_convert_fusion.2
  215.7 1.7 collective-permute-start.39
  219.7 10.7 %collective-permute-done.37 = bf16[128,1024]{1,0:T(8,128)(2,1)S(1)} collective-permute-done((bf16[128,1024]{1,0:T(8,128)(2,1)S(1)}, bf16[128,1024]{1,0:T(8,128)(2,1)S(1)}, u32[]{:S(2)}, u32[]{:S(2)}) %collective-permute-start.37) | collective-permute-done | bytes 262176 | tf_op jit(solution)/shard_map/ppermute | solution.py:46
  233.2 2.3 collective-permute-start.41
  236.3 2.7 collective-permute-start.45
  240.8 6.8 %collective-permute-done.41 = bf16[128,1024]{1,0:T(8,128)(2,1)S(1)} collective-permute-done((bf16[128,1024]{1,0:T(8,128)(2,1)S(1)}, bf16[128,1024]{1,0:T(8,128)(2,1)S(1)}, u32[]{:S(2)}, u32[]{:S(2)}) %collective-permute-start.41) | collective-permute-done | bytes 262176 | tf_op jit(solution)/shard_map/ppermute | solution.py:46
  249.6 2.2 collective-permute-done.44
  251.8 10.4 %collective-permute-done.46 = bf16[2,2,64,1152]{3,2,1,0:T(8,128)(2,1)S(1)} collective-permute-done((bf16[2,2,64,1152]{3,2,1,0:T(8,128)(2,1)S(1)}, bf16[2,2,64,1152]{3,2,1,0:T(8,128)(2,1)S(1)}, u32[]{:S(2)}, u32[]{:S(2)}) %collective-permute-start.46) | collective-permute-done | bytes 589856 | tf_op jit(solution)/shard_map/ppermute | solution.py:46
  262.8 3.7 collective-permute-start.47
  268.0 3.3 collective-permute-start.53
  272.0 1.8 collective-permute-done.51
  273.8 4.0 %collective-permute-done.53 = bf16[2,2,64,256]{3,2,1,0:T(8,128)(2,1)S(1)} collective-permute-done((bf16[2,2,64,256]{3,2,1,0:T(8,128)(2,1)S(1)}, bf16[2,2,64,256]{3,2,1,0:T(8,128)(2,1)S(1)}, u32[]{:S(2)}, u32[]{:S(2)}) %collective-permute-start.53) | collective-permute-done | bytes 131104 | tf_op jit(solution)/shard_map/ppermute | solution.py:46
  277.9 1.9 collective-permute-start.54
  279.9 5.4 %collective-permute-start.56 = (bf16[64,1408]{1,0:T(8,128)(2,1)S(1)}, bf16[64,1408]{1,0:T(8,128)(2,1)S(1)}, u32[]{:S(2)}, u32[]{:S(2)}) collective-permute-start(bf16[64,1408]{1,0:T(8,128)(2,1)S(1)} %get-tuple-element.117), channel_id=1, source_target_pairs={{4,0},{6,8},{20,16},{22,24},{36,32},{38,40},{52,48},{54,56},{12,2}... | collective-permute-start | bytes 540680 | tf_op jit(solution)/shard_map/ppermute | solution.py:147
  286.7 19.3 %attend_back.1 = (f32[1024,256]{1,0:T(8,128)}, bf16[1024,256]{1,0:T(8,128)(2,1)S(1)}, bf16[1024,256]{1,0:T(8,128)(2,1)S(1)}, bf16[1024,256]{1,0:T(8,128)(2,1)S(1)}, bf16[1024,256]{1,0:T(8,128)(2,1)S(1)}) custom-call(s32[32]{0:T(128)S(1)} %select_reduce_fusion.1.kblk, s32[8]{0:T(128)S(1)} %get-tuple-element.144.qblk, s32[8]{0:T(128)S(1)} %and_select_fusion.3.low, ...), custom_call_target="tpu_custom_call" | custom-call | flops 20000000000 | bytes 20000000 | tf_op jit(solution)/shard_map/attend_back/pallas_call | solution.py:384
  306.0 2.7 collective-permute-start.59
  311.5 6.3 %collective-permute-done.50 = bf16[128,1024]{1,0:T(8,128)(2,1)S(1)} collective-permute-done((bf16[128,1024]{1,0:T(8,128)(2,1)S(1)}, bf16[128,1024]{1,0:T(8,128)(2,1)S(1)}, u32[]{:S(2)}, u32[]{:S(2)}) %collective-permute-start.50) | collective-permute-done | bytes 262176 | tf_op jit(solution)/shard_map/ppermute | solution.py:46
  317.8 4.8 %collective-permute-done.49 = bf16[128,1024]{1,0:T(8,128)(2,1)S(1)} collective-permute-done((bf16[128,1024]{1,0:T(8,128)(2,1)S(1)}, bf16[128,1024]{1,0:T(8,128)(2,1)S(1)}, u32[]{:S(2)}, u32[]{:S(2)}) %collective-permute-start.49) | collective-permute-done | bytes 262176 | tf_op jit(solution)/shard_map/ppermute | solution.py:46
  323.5 8.6 %collective-permute-done.58.kv1 = bf16[1024,256]{1,0:T(8,128)(2,1)S(1)} collective-permute-done((bf16[1024,256]{1,0:T(8,128)(2,1)S(1)}, bf16[1024,256]{1,0:T(8,128)(2,1)S(1)}, u32[]{:S(2)}, u32[]{:S(2)}) %collective-permute-start.58) | collective-permute-done | bytes 524320 | tf_op jit(solution)/shard_map/ppermute | solution.py:46
  332.1 8.6 %project_back.1 = (bf16[1024,512]{1,0:T(8,128)(2,1)S(1)}, bf16[1024,1024]{1,0:T(8,128)(2,1)}, f32[8,1024]{1,0:T(8,128)S(1)}, f32[8,128]{1,0:T(8,128)S(1)}, f32[8,128]{1,0:T(8,128)S(1)}) custom-call(f32[1024,256]{1,0:T(8,128)S(1)} %copy-done.13, bf16[1024,256]{1,0:T(8,128)(2,1)S(1)} %get-tuple-element.69.kv0, ...), custom_call_target="tpu_custom_call" | custom-call | flops 8999999488 | bytes 9000000 | tf_op jit(solution)/shard_map/project_back/pallas_call | solution.py:238
  348.8 2.7 collective-permute-start.70
  353.1 2.3 collective-permute-done.69
  357.1 2.4 collective-permute-done.74
  363.9 4.8 %collective-permute-done.77 = bf16[2,2,64,512]{3,2,1,0:T(8,128)(2,1)S(1)} collective-permute-done((bf16[2,2,64,512]{3,2,1,0:T(8,128)(2,1)S(1)}, bf16[2,2,64,512]{3,2,1,0:T(8,128)(2,1)S(1)}, u32[]{:S(2)}, u32[]{:S(2)}) %collective-permute-start.77) | collective-permute-done | bytes 262176 | tf_op jit(solution)/shard_map/ppermute | solution.py:46
  368.9 7.5 %collective-permute-start.78 = (bf16[64,512]{1,0:T(8,128)(2,1)S(1)}, bf16[64,512]{1,0:T(8,128)(2,1)S(1)}, u32[]{:S(2)}, u32[]{:S(2)}) collective-permute-start(bf16[64,512]{1,0:T(8,128)(2,1)S(1)} %get-tuple-element.125), channel_id=1, source_target_pairs={{0,0},{2,8},{16,16},{18,24},{32,32},{34,40},{48,48},{50,56},{8,2},... | collective-permute-start | bytes 196616 | tf_op jit(solution)/shard_map/ppermute | solution.py:147
  379.4 2.3 collective-permute-start.62
  381.7 2.4 collective-permute-start.64
  387.8 8.7 %collective-permute-done.64 = bf16[128,1024]{1,0:T(8,128)(2,1)S(1)} collective-permute-done((bf16[128,1024]{1,0:T(8,128)(2,1)S(1)}, bf16[128,1024]{1,0:T(8,128)(2,1)S(1)}, u32[]{:S(2)}, u32[]{:S(2)}) %collective-permute-start.64) | collective-permute-done | bytes 262176 | tf_op jit(solution)/shard_map/ppermute | solution.py:46
  (313 shorter events, 85.9 us)
Async XLA Ops:
  5.4 21.0 %collective-permute-start.7 = (bf16[64,640]{1,0:T(8,128)(2,1)}, bf16[64,640]{1,0:T(8,128)(2,1)}, u32[]{:S(2)}, u32[]{:S(2)}) collective-permute-start(bf16[64,640]{1,0:T(8,128)(2,1)} %concatenate.80), channel_id=1, source_target_pairs={{0,6},{8,0},{16,22},{24,16},{32,38},{40,32},{48,54},{56,48},{2,14}... | collective-permute-start | bytes 245768 | tf_op jit(solution)/shard_map/ppermute | solution.py:103
  6.8 18.7 %collective-permute-start.6 = (bf16[64,640]{1,0:T(8,128)(2,1)}, bf16[64,640]{1,0:T(8,128)(2,1)}, u32[]{:S(2)}, u32[]{:S(2)}) collective-permute-start(bf16[64,640]{1,0:T(8,128)(2,1)} %concatenate.80), channel_id=1, source_target_pairs={{0,4},{8,6},{16,20},{24,22},{32,36},{40,38},{48,52},{56,54},{2,12}... | collective-permute-start | bytes 245768 | tf_op jit(solution)/shard_map/ppermute | solution.py:103
  10.4 12.7 %collective-permute-start.5 = (bf16[64,640]{1,0:T(8,128)(2,1)}, bf16[64,640]{1,0:T(8,128)(2,1)}, u32[]{:S(2)}, u32[]{:S(2)}) collective-permute-start(bf16[64,640]{1,0:T(8,128)(2,1)} %concatenate.80), channel_id=1, source_target_pairs={{0,2},{8,4},{16,18},{24,20},{32,34},{40,36},{48,50},{56,52},{2,10}... | collective-permute-start | bytes 245768 | tf_op jit(solution)/shard_map/ppermute | solution.py:103
  11.9 9.8 %collective-permute-start.4 = (bf16[64,640]{1,0:T(8,128)(2,1)}, bf16[64,640]{1,0:T(8,128)(2,1)S(1)}, u32[]{:S(2)}, u32[]{:S(2)}) collective-permute-start(bf16[64,640]{1,0:T(8,128)(2,1)} %concatenate.80), channel_id=1, source_target_pairs={{0,0},{8,2},{16,16},{24,18},{32,32},{40,34},{48,48},{56,50},{2,8},... | collective-permute-start | bytes 245768 | tf_op jit(solution)/shard_map/ppermute | solution.py:103
  13.8 42.8 %collective-permute-start.2 = (bf16[128,1024]{1,0:T(8,128)(2,1)}, bf16[128,1024]{1,0:T(8,128)(2,1)S(1)}, u32[]{:S(2)}, u32[]{:S(2)}) collective-permute-start(bf16[128,1024]{1,0:T(8,128)(2,1)} %param.16), channel_id=1, source_target_pairs={{0,1},{8,9},{16,17},{24,25},{32,33},{40,41},{48,49},{56,57},{2,3},... | collective-permute-start | bytes 786440 | tf_op jit(solution)/shard_map/ppermute | solution.py:46
  21.7 35.6 %collective-permute-start.1 = (bf16[128,1024]{1,0:T(8,128)(2,1)S(1)}, bf16[128,1024]{1,0:T(8,128)(2,1)S(1)}, u32[]{:S(2)}, u32[]{:S(2)}) collective-permute-start(bf16[128,1024]{1,0:T(8,128)(2,1)S(1)} %copy-done.17), channel_id=1, source_target_pairs={{0,64},{8,72},{16,80},{24,88},{32,96},{40,104},{48,112},{56,120},{... | collective-permute-start | bytes 786440 | tf_op jit(solution)/shard_map/ppermute | solution.py:46
  23.1 29.1 %collective-permute-start = (bf16[128,1024]{1,0:T(8,128)(2,1)S(1)}, bf16[128,1024]{1,0:T(8,128)(2,1)S(1)}, u32[]{:S(2)}, u32[]{:S(2)}) collective-permute-start(bf16[128,1024]{1,0:T(8,128)(2,1)S(1)} %copy-done.17), channel_id=1, source_target_pairs={{0,65},{8,73},{16,81},{24,89},{32,97},{40,105},{48,113},{56,121},{... | collective-permute-start | bytes 786440 | tf_op jit(solution)/shard_map/ppermute | solution.py:46
  32.8 29.3 %collective-permute-start.11 = (bf16[64,1408]{1,0:T(8,128)(2,1)}, bf16[64,1408]{1,0:T(8,128)(2,1)S(1)}, u32[]{:S(2)}, u32[]{:S(2)}) collective-permute-start(bf16[64,1408]{1,0:T(8,128)(2,1)} %pad_maximum_fusion.9), channel_id=1, source_target_pairs={{0,6},{8,0},{16,22},{24,16},{32,38},{40,32},{48,54},{56,48},{2,14}... | collective-permute-start | bytes 540680 | tf_op jit(solution)/shard_map/ppermute | solution.py:103
  35.3 12.0 %collective-permute-start.9 = (bf16[64,1408]{1,0:T(8,128)(2,1)}, bf16[64,1408]{1,0:T(8,128)(2,1)S(1)}, u32[]{:S(2)}, u32[]{:S(2)}) collective-permute-start(bf16[64,1408]{1,0:T(8,128)(2,1)} %pad_maximum_fusion.9), channel_id=1, source_target_pairs={{0,2},{8,4},{16,18},{24,20},{32,34},{40,36},{48,50},{56,52},{2,10}... | collective-permute-start | bytes 540680 | tf_op jit(solution)/shard_map/ppermute | solution.py:103
  47.3 13.0 %collective-permute-start.10 = (bf16[64,1408]{1,0:T(8,128)(2,1)}, bf16[64,1408]{1,0:T(8,128)(2,1)S(1)}, u32[]{:S(2)}, u32[]{:S(2)}) collective-permute-start(bf16[64,1408]{1,0:T(8,128)(2,1)} %pad_maximum_fusion.9), channel_id=1, source_target_pairs={{0,4},{8,6},{16,20},{24,22},{32,36},{40,38},{48,52},{56,54},{2,12}... | collective-permute-start | bytes 540680 | tf_op jit(solution)/shard_map/ppermute | solution.py:103
  52.2 11.6 %collective-permute-start.14 = (bf16[256,640]{1,0:T(8,128)(2,1)S(1)}, bf16[256,640]{1,0:T(8,128)(2,1)S(1)}, u32[]{:S(2)}, u32[]{:S(2)}) collective-permute-start(bf16[256,640]{1,0:T(8,128)(2,1)S(1)} %constant_dynamic-update-slice_fusion.5.refs_0_), channel_id=1, source_target_pairs={{0,32},{8,40},{16,48},{24,56},{32,0},{40,8},{48,16},{56,24},{2,34}... | collective-permute-start | bytes 983048 | tf_op jit(solution)/shard_map/ppermute | solution.py:46
  56.6 14.1 %collective-permute-start.13 = (bf16[256,640]{1,0:T(8,128)(2,1)S(1)}, bf16[256,640]{1,0:T(8,128)(2,1)S(1)}, u32[]{:S(2)}, u32[]{:S(2)}) collective-permute-start(bf16[256,640]{1,0:T(8,128)(2,1)S(1)} %constant_dynamic-update-slice_fusion.5.refs_0_), channel_id=1, source_target_pairs={{0,16},{8,24},{16,32},{24,40},{32,48},{40,56},{48,0},{56,8},{2,18}... | collective-permute-start | bytes 983048 | tf_op jit(solution)/shard_map/ppermute | solution.py:46
  57.3 14.4 %collective-permute-start.12 = (bf16[256,640]{1,0:T(8,128)(2,1)S(1)}, bf16[256,640]{1,0:T(8,128)(2,1)S(1)}, u32[]{:S(2)}, u32[]{:S(2)}) collective-permute-start(bf16[256,640]{1,0:T(8,128)(2,1)S(1)} %constant_dynamic-update-slice_fusion.5.refs_0_), channel_id=1, source_target_pairs={{0,48},{8,56},{16,0},{24,8},{32,16},{40,24},{48,32},{56,40},{2,50}... | collective-permute-start | bytes 983048 | tf_op jit(solution)/shard_map/ppermute | solution.py:46
  60.3 12.6 %collective-permute-start.3 = (bf16[512,1024]{1,0:T(8,128)(2,1)}, bf16[512,1024]{1,0:T(8,128)(2,1)}, u32[]{:S(2)}, u32[]{:S(2)}) collective-permute-start(bf16[512,1024]{1,0:T(8,128)(2,1)} %pad_maximum_fusion.1), channel_id=1, source_target_pairs={{0,8},{8,0},{16,24},{24,16},{32,40},{40,32},{48,56},{56,48},{2,10}... | collective-permute-start | bytes 3145736 | tf_op jit(solution)/shard_map/ppermute | solution.py:46
  83.2 14.7 %collective-permute-start.21 = (bf16[1024,256]{1,0:T(8,128)(2,1)S(1)}, bf16[1024,256]{1,0:T(8,128)(2,1)S(1)}, u32[]{:S(2)}, u32[]{:S(2)}) collective-permute-start(bf16[1024,256]{1,0:T(8,128)(2,1)S(1)} %get-tuple-element.52.kv0), channel_id=1, source_target_pairs={{0,32},{8,40},{16,48},{24,56},{32,0},{40,8},{48,16},{56,24},{2,34}... | collective-permute-start | bytes 1572872 | tf_op jit(solution)/shard_map/ppermute | solution.py:46
  85.5 24.3 %collective-permute-start.20 = (bf16[1024,256]{1,0:T(8,128)(2,1)S(1)}, bf16[1024,256]{1,0:T(8,128)(2,1)S(1)}, u32[]{:S(2)}, u32[]{:S(2)}) collective-permute-start(bf16[1024,256]{1,0:T(8,128)(2,1)S(1)} %get-tuple-element.52.kv0), channel_id=1, source_target_pairs={{0,16},{8,24},{16,32},{24,40},{32,48},{40,56},{48,0},{56,8},{2,18}... | collective-permute-start | bytes 1572872 | tf_op jit(solution)/shard_map/ppermute | solution.py:46
  86.2 23.6 %collective-permute-start.19 = (bf16[1024,256]{1,0:T(8,128)(2,1)S(1)}, bf16[1024,256]{1,0:T(8,128)(2,1)S(1)}, u32[]{:S(2)}, u32[]{:S(2)}) collective-permute-start(bf16[1024,256]{1,0:T(8,128)(2,1)S(1)} %get-tuple-element.52.kv0), channel_id=1, source_target_pairs={{0,48},{8,56},{16,0},{24,8},{32,16},{40,24},{48,32},{56,40},{2,50}... | collective-permute-start | bytes 1572872 | tf_op jit(solution)/shard_map/ppermute | solution.py:46
  109.8 18.7 %collective-permute-start.24 = (bf16[256,256]{1,0:T(8,128)(2,1)S(1)}, bf16[256,256]{1,0:T(8,128)(2,1)S(1)}, u32[]{:S(2)}, u32[]{:S(2)}) collective-permute-start(bf16[256,256]{1,0:T(8,128)(2,1)S(1)} %slice.182.refs_0_), channel_id=1, source_target_pairs={{0,32},{8,40},{16,48},{24,56},{32,0},{40,8},{48,16},{56,24},{2,34}... | collective-permute-start | bytes 393224 | tf_op jit(solution)/shard_map/ppermute | solution.py:46
  111.2 17.3 %collective-permute-start.23 = (bf16[256,256]{1,0:T(8,128)(2,1)S(1)}, bf16[256,256]{1,0:T(8,128)(2,1)S(1)}, u32[]{:S(2)}, u32[]{:S(2)}) collective-permute-start(bf16[256,256]{1,0:T(8,128)(2,1)S(1)} %slice.182.refs_0_), channel_id=1, source_target_pairs={{0,16},{8,24},{16,32},{24,40},{32,48},{40,56},{48,0},{56,8},{2,18}... | collective-permute-start | bytes 393224 | tf_op jit(solution)/shard_map/ppermute | solution.py:46
  112.8 15.7 %collective-permute-start.22 = (bf16[256,256]{1,0:T(8,128)(2,1)S(1)}, bf16[256,256]{1,0:T(8,128)(2,1)S(1)}, u32[]{:S(2)}, u32[]{:S(2)}) collective-permute-start(bf16[256,256]{1,0:T(8,128)(2,1)S(1)} %slice.182.refs_0_), channel_id=1, source_target_pairs={{0,48},{8,56},{16,0},{24,8},{32,16},{40,24},{48,32},{56,40},{2,50}... | collective-permute-start | bytes 393224 | tf_op jit(solution)/shard_map/ppermute | solution.py:46
  134.9 20.0 %collective-permute-start.29 = (bf16[128,1024]{1,0:T(8,128)(2,1)S(1)}, bf16[128,1024]{1,0:T(8,128)(2,1)S(1)}, u32[]{:S(2)}, u32[]{:S(2)}) collective-permute-start(bf16[128,1024]{1,0:T(8,128)(2,1)S(1)} %get-tuple-element.112), channel_id=1, source_target_pairs={{0,64},{8,72},{16,80},{24,88},{32,96},{40,104},{48,112},{56,120},{... | collective-permute-start | bytes 786440 | tf_op jit(solution)/shard_map/ppermute | solution.py:46
  135.0 20.0 %collective-permute-start.31 = (bf16[128,1024]{1,0:T(8,128)(2,1)S(1)}, bf16[128,1024]{1,0:T(8,128)(2,1)S(1)}, u32[]{:S(2)}, u32[]{:S(2)}) collective-permute-start(bf16[128,1024]{1,0:T(8,128)(2,1)S(1)} %get-tuple-element.113), channel_id=1, source_target_pairs={{0,1},{8,9},{16,17},{24,25},{32,33},{40,41},{48,49},{56,57},{2,3},... | collective-permute-start | bytes 786440 | tf_op jit(solution)/shard_map/ppermute | solution.py:46
  135.1 19.9 %collective-permute-start.30 = (bf16[128,1024]{1,0:T(8,128)(2,1)S(1)}, bf16[128,1024]{1,0:T(8,128)(2,1)S(1)}, u32[]{:S(2)}, u32[]{:S(2)}) collective-permute-start(bf16[128,1024]{1,0:T(8,128)(2,1)S(1)} %get-tuple-element.114), channel_id=1, source_target_pairs={{0,65},{8,73},{16,81},{24,89},{32,97},{40,105},{48,113},{56,121},{... | collective-permute-start | bytes 786440 | tf_op jit(solution)/shard_map/ppermute | solution.py:46
  137.7 20.0 %collective-permute-start.17 = (bf16[128,1024]{1,0:T(8,128)(2,1)S(1)}, bf16[128,1024]{1,0:T(8,128)(2,1)S(1)}, u32[]{:S(2)}, u32[]{:S(2)}) collective-permute-start(bf16[128,1024]{1,0:T(8,128)(2,1)S(1)} %copy-done.18), channel_id=1, source_target_pairs={{0,1},{8,9},{16,17},{24,25},{32,33},{40,41},{48,49},{56,57},{2,3},... | collective-permute-start | bytes 786440 | tf_op jit(solution)/shard_map/ppermute | solution.py:46
  140.0 23.8 %collective-permute-start.16 = (bf16[128,1024]{1,0:T(8,128)(2,1)S(1)}, bf16[128,1024]{1,0:T(8,128)(2,1)S(1)}, u32[]{:S(2)}, u32[]{:S(2)}) collective-permute-start(bf16[128,1024]{1,0:T(8,128)(2,1)S(1)} %copy-done.18), channel_id=1, source_target_pairs={{0,64},{8,72},{16,80},{24,88},{32,96},{40,104},{48,112},{56,120},{... | collective-permute-start | bytes 786440 | tf_op jit(solution)/shard_map/ppermute | solution.py:46
  155.0 8.9 %collective-permute-start.15 = (bf16[128,1024]{1,0:T(8,128)(2,1)S(1)}, bf16[128,1024]{1,0:T(8,128)(2,1)S(1)}, u32[]{:S(2)}, u32[]{:S(2)}) collective-permute-start(bf16[128,1024]{1,0:T(8,128)(2,1)S(1)} %copy-done.18), channel_id=1, source_target_pairs={{0,65},{8,73},{16,81},{24,89},{32,97},{40,105},{48,113},{56,121},{... | collective-permute-start | bytes 786440 | tf_op jit(solution)/shard_map/ppermute | solution.py:46
  156.2 11.9 %collective-permute-start.34 = (bf16[128,1024]{1,0:T(8,128)(2,1)S(1)}, bf16[128,1024]{1,0:T(8,128)(2,1)S(1)}, u32[]{:S(2)}, u32[]{:S(2)}) collective-permute-start(bf16[128,1024]{1,0:T(8,128)(2,1)S(1)} %get-tuple-element.89), channel_id=1, source_target_pairs={{0,1},{8,9},{16,17},{24,25},{32,33},{40,41},{48,49},{56,57},{2,3},... | collective-permute-start | bytes 786440 | tf_op jit(solution)/shard_map/ppermute | solution.py:46
  156.2 15.6 %collective-permute-start.33 = (bf16[128,1024]{1,0:T(8,128)(2,1)S(1)}, bf16[128,1024]{1,0:T(8,128)(2,1)S(1)}, u32[]{:S(2)}, u32[]{:S(2)}) collective-permute-start(bf16[128,1024]{1,0:T(8,128)(2,1)S(1)} %get-tuple-element.89), channel_id=1, source_target_pairs={{0,64},{8,72},{16,80},{24,88},{32,96},{40,104},{48,112},{56,120},{... | collective-permute-start | bytes 786440 | tf_op jit(solution)/shard_map/ppermute | solution.py:46
  157.6 14.4 %collective-permute-start.32 = (bf16[128,1024]{1,0:T(8,128)(2,1)S(1)}, bf16[128,1024]{1,0:T(8,128)(2,1)S(1)}, u32[]{:S(2)}, u32[]{:S(2)}) collective-permute-start(bf16[128,1024]{1,0:T(8,128)(2,1)S(1)} %get-tuple-element.89), channel_id=1, source_target_pairs={{0,65},{8,73},{16,81},{24,89},{32,97},{40,105},{48,113},{56,121},{... | collective-permute-start | bytes 786440 | tf_op jit(solution)/shard_map/ppermute | solution.py:46
  163.9 33.8 %collective-permute-start.18 = (bf16[512,1024]{1,0:T(8,128)(2,1)S(1)}, bf16[512,1024]{1,0:T(8,128)(2,1)S(1)}, u32[]{:S(2)}, u32[]{:S(2)}) collective-permute-start(bf16[512,1024]{1,0:T(8,128)(2,1)S(1)} %pad_maximum_fusion.2), channel_id=1, source_target_pairs={{0,8},{8,0},{16,24},{24,16},{32,40},{40,32},{48,56},{56,48},{2,10}... | collective-permute-start | bytes 3145736 | tf_op jit(solution)/shard_map/ppermute | solution.py:46
  167.6 16.4 %collective-permute-start.27 = (bf16[256,1152]{1,0:T(8,128)(2,1)S(1)}, bf16[256,1152]{1,0:T(8,128)(2,1)S(1)}, u32[]{:S(2)}, u32[]{:S(2)}) collective-permute-start(bf16[256,1152]{1,0:T(8,128)(2,1)S(1)} %slice.183.refs_0_), channel_id=1, source_target_pairs={{0,32},{8,40},{16,48},{24,56},{32,0},{40,8},{48,16},{56,24},{2,34}... | collective-permute-start | bytes 1769480 | tf_op jit(solution)/shard_map/ppermute | solution.py:46
  168.0 29.0 %collective-permute-start.26 = (bf16[256,1152]{1,0:T(8,128)(2,1)S(1)}, bf16[256,1152]{1,0:T(8,128)(2,1)S(1)}, u32[]{:S(2)}, u32[]{:S(2)}) collective-permute-start(bf16[256,1152]{1,0:T(8,128)(2,1)S(1)} %slice.183.refs_0_), channel_id=1, source_target_pairs={{0,16},{8,24},{16,32},{24,40},{32,48},{40,56},{48,0},{56,8},{2,18}... | collective-permute-start | bytes 1769480 | tf_op jit(solution)/shard_map/ppermute | solution.py:46
  171.8 25.2 %collective-permute-start.25 = (bf16[256,1152]{1,0:T(8,128)(2,1)S(1)}, bf16[256,1152]{1,0:T(8,128)(2,1)S(1)}, u32[]{:S(2)}, u32[]{:S(2)}) collective-permute-start(bf16[256,1152]{1,0:T(8,128)(2,1)S(1)} %slice.183.refs_0_), channel_id=1, source_target_pairs={{0,48},{8,56},{16,0},{24,8},{32,16},{40,24},{48,32},{56,40},{2,50}... | collective-permute-start | bytes 1769480 | tf_op jit(solution)/shard_map/ppermute | solution.py:46
  172.1 28.4 %collective-permute-start.35 = (bf16[512,1024]{1,0:T(8,128)(2,1)S(1)}, bf16[512,1024]{1,0:T(8,128)(2,1)S(1)}, u32[]{:S(2)}, u32[]{:S(2)}) collective-permute-start(bf16[512,1024]{1,0:T(8,128)(2,1)S(1)} %pad_maximum_fusion.3), channel_id=1, source_target_pairs={{0,8},{8,0},{16,24},{24,16},{32,40},{40,32},{48,56},{56,48},{2,10}... | collective-permute-start | bytes 3145736 | tf_op jit(solution)/shard_map/ppermute | solution.py:46
  215.6 14.8 %collective-permute-start.37 = (bf16[128,1024]{1,0:T(8,128)(2,1)S(1)}, bf16[128,1024]{1,0:T(8,128)(2,1)S(1)}, u32[]{:S(2)}, u32[]{:S(2)}) collective-permute-start(bf16[128,1024]{1,0:T(8,128)(2,1)S(1)} %get-tuple-element.109), channel_id=1, source_target_pairs={{0,64},{8,72},{16,80},{24,88},{32,96},{40,104},{48,112},{56,120},{... | collective-permute-start | bytes 786440 | tf_op jit(solution)/shard_map/ppermute | solution.py:46
  215.7 14.7 %collective-permute-start.39 = (bf16[128,1024]{1,0:T(8,128)(2,1)S(1)}, bf16[128,1024]{1,0:T(8,128)(2,1)S(1)}, u32[]{:S(2)}, u32[]{:S(2)}) collective-permute-start(bf16[128,1024]{1,0:T(8,128)(2,1)S(1)} %get-tuple-element.110), channel_id=1, source_target_pairs={{0,1},{8,9},{16,17},{24,25},{32,33},{40,41},{48,49},{56,57},{2,3},... | collective-permute-start | bytes 786440 | tf_op jit(solution)/shard_map/ppermute | solution.py:46
  217.4 13.3 %collective-permute-start.38 = (bf16[128,1024]{1,0:T(8,128)(2,1)S(1)}, bf16[128,1024]{1,0:T(8,128)(2,1)S(1)}, u32[]{:S(2)}, u32[]{:S(2)}) collective-permute-start(bf16[128,1024]{1,0:T(8,128)(2,1)S(1)} %get-tuple-element.111), channel_id=1, source_target_pairs={{0,65},{8,73},{16,81},{24,89},{32,97},{40,105},{48,113},{56,121},{... | collective-permute-start | bytes 786440 | tf_op jit(solution)/shard_map/ppermute | solution.py:46
  232.2 8.2 %collective-permute-start.42 = (bf16[128,1024]{1,0:T(8,128)(2,1)S(1)}, bf16[128,1024]{1,0:T(8,128)(2,1)S(1)}, u32[]{:S(2)}, u32[]{:S(2)}) collective-permute-start(bf16[128,1024]{1,0:T(8,128)(2,1)S(1)} %get-tuple-element.86), channel_id=1, source_target_pairs={{0,1},{8,9},{16,17},{24,25},{32,33},{40,41},{48,49},{56,57},{2,3},... | collective-permute-start | bytes 786440 | tf_op jit(solution)/shard_map/ppermute | solution.py:46
  233.2 14.4 %collective-permute-start.41 = (bf16[128,1024]{1,0:T(8,128)(2,1)S(1)}, bf16[128,1024]{1,0:T(8,128)(2,1)S(1)}, u32[]{:S(2)}, u32[]{:S(2)}) collective-permute-start(bf16[128,1024]{1,0:T(8,128)(2,1)S(1)} %get-tuple-element.86), channel_id=1, source_target_pairs={{0,64},{8,72},{16,80},{24,88},{32,96},{40,104},{48,112},{56,120},{... | collective-permute-start | bytes 786440 | tf_op jit(solution)/shard_map/ppermute | solution.py:46
  235.4 12.2 %collective-permute-start.40 = (bf16[128,1024]{1,0:T(8,128)(2,1)S(1)}, bf16[128,1024]{1,0:T(8,128)(2,1)S(1)}, u32[]{:S(2)}, u32[]{:S(2)}) collective-permute-start(bf16[128,1024]{1,0:T(8,128)(2,1)S(1)} %get-tuple-element.86), channel_id=1, source_target_pairs={{0,65},{8,73},{16,81},{24,89},{32,97},{40,105},{48,113},{56,121},{... | collective-permute-start | bytes 786440 | tf_op jit(solution)/shard_map/ppermute | solution.py:46
  236.3 15.6 %collective-permute-start.44 = (bf16[2,2,64,1152]{3,2,1,0:T(8,128)(2,1)S(1)}, bf16[2,2,64,1152]{3,2,1,0:T(8,128)(2,1)S(1)}, u32[]{:S(2)}, u32[]{:S(2)}) collective-permute-start(bf16[2,2,64,1152]{3,2,1,0:T(8,128)(2,1)S(1)} %get-tuple-element.97), channel_id=1, source_target_pairs={{0,16},{8,24},{16,32},{24,40},{32,48},{40,56},{48,0},{56,8},{2,18}... | collective-permute-start | bytes 1769480 | tf_op jit(solution)/shard_map/ppermute | solution.py:46
  236.3 15.5 %collective-permute-start.45 = (bf16[2,2,64,1152]{3,2,1,0:T(8,128)(2,1)S(1)}, bf16[2,2,64,1152]{3,2,1,0:T(8,128)(2,1)S(1)}, u32[]{:S(2)}, u32[]{:S(2)}) collective-permute-start(bf16[2,2,64,1152]{3,2,1,0:T(8,128)(2,1)S(1)} %get-tuple-element.98), channel_id=1, source_target_pairs={{0,48},{8,56},{16,0},{24,8},{32,16},{40,24},{48,32},{56,40},{2,50}... | collective-permute-start | bytes 1769480 | tf_op jit(solution)/shard_map/ppermute | solution.py:46
  240.5 21.8 %collective-permute-start.46 = (bf16[2,2,64,1152]{3,2,1,0:T(8,128)(2,1)S(1)}, bf16[2,2,64,1152]{3,2,1,0:T(8,128)(2,1)S(1)}, u32[]{:S(2)}, u32[]{:S(2)}) collective-permute-start(bf16[2,2,64,1152]{3,2,1,0:T(8,128)(2,1)S(1)} %get-tuple-element.99), channel_id=1, source_target_pairs={{0,32},{8,40},{16,48},{24,56},{32,0},{40,8},{48,16},{56,24},{2,34}... | collective-permute-start | bytes 1769480 | tf_op jit(solution)/shard_map/ppermute | solution.py:46
  247.7 15.0 %collective-permute-start.43 = (bf16[512,1024]{1,0:T(8,128)(2,1)S(1)}, bf16[512,1024]{1,0:T(8,128)(2,1)S(1)}, u32[]{:S(2)}, u32[]{:S(2)}) collective-permute-start(bf16[512,1024]{1,0:T(8,128)(2,1)S(1)} %pad_maximum_fusion.4), channel_id=1, source_target_pairs={{0,8},{8,0},{16,24},{24,16},{32,40},{40,32},{48,56},{56,48},{2,10}... | collective-permute-start | bytes 3145736 | tf_op jit(solution)/shard_map/ppermute | solution.py:46
  262.8 22.5 %collective-permute-start.47 = (bf16[512,1024]{1,0:T(8,128)(2,1)S(1)}, bf16[512,1024]{1,0:T(8,128)(2,1)S(1)}, u32[]{:S(2)}, u32[]{:S(2)}) collective-permute-start(bf16[512,1024]{1,0:T(8,128)(2,1)S(1)} %slice.158), channel_id=1, source_target_pairs={{0,8},{8,0},{16,24},{24,16},{32,40},{40,32},{48,56},{56,48},{2,10}... | collective-permute-start | bytes 3145736 | tf_op jit(solution)/shard_map/ppermute | solution.py:46
  268.0 9.7 %collective-permute-start.53 = (bf16[2,2,64,256]{3,2,1,0:T(8,128)(2,1)S(1)}, bf16[2,2,64,256]{3,2,1,0:T(8,128)(2,1)S(1)}, u32[]{:S(2)}, u32[]{:S(2)}) collective-permute-start(bf16[2,2,64,256]{3,2,1,0:T(8,128)(2,1)S(1)} %get-tuple-element.120), channel_id=1, source_target_pairs={{0,32},{8,40},{16,48},{24,56},{32,0},{40,8},{48,16},{56,24},{2,34}... | collective-permute-start | bytes 393224 | tf_op jit(solution)/shard_map/ppermute | solution.py:46
  277.9 28.1 %collective-permute-start.54 = (bf16[64,1408]{1,0:T(8,128)(2,1)S(1)}, bf16[64,1408]{1,0:T(8,128)(2,1)S(1)}, u32[]{:S(2)}, u32[]{:S(2)}) collective-permute-start(bf16[64,1408]{1,0:T(8,128)(2,1)S(1)} %get-tuple-element.115), channel_id=1, source_target_pairs={{0,0},{2,8},{16,16},{18,24},{32,32},{34,40},{48,48},{50,56},{8,2},... | collective-permute-start | bytes 540680 | tf_op jit(solution)/shard_map/ppermute | solution.py:147
  279.9 26.1 %collective-permute-start.55 = (bf16[64,1408]{1,0:T(8,128)(2,1)S(1)}, bf16[64,1408]{1,0:T(8,128)(2,1)S(1)}, u32[]{:S(2)}, u32[]{:S(2)}) collective-permute-start(bf16[64,1408]{1,0:T(8,128)(2,1)S(1)} %get-tuple-element.116), channel_id=1, source_target_pairs={{2,0},{4,8},{18,16},{20,24},{34,32},{36,40},{50,48},{52,56},{10,2}... | collective-permute-start | bytes 540680 | tf_op jit(solution)/shard_map/ppermute | solution.py:147
  279.9 28.7 %collective-permute-start.56 = (bf16[64,1408]{1,0:T(8,128)(2,1)S(1)}, bf16[64,1408]{1,0:T(8,128)(2,1)S(1)}, u32[]{:S(2)}, u32[]{:S(2)}) collective-permute-start(bf16[64,1408]{1,0:T(8,128)(2,1)S(1)} %get-tuple-element.117), channel_id=1, source_target_pairs={{4,0},{6,8},{20,16},{22,24},{36,32},{38,40},{52,48},{54,56},{12,2}... | collective-permute-start | bytes 540680 | tf_op jit(solution)/shard_map/ppermute | solution.py:147
  285.3 23.4 %collective-permute-start.57 = (bf16[64,1408]{1,0:T(8,128)(2,1)S(1)}, bf16[64,1408]{1,0:T(8,128)(2,1)S(1)}, u32[]{:S(2)}, u32[]{:S(2)}) collective-permute-start(bf16[64,1408]{1,0:T(8,128)(2,1)S(1)} %get-tuple-element.118), channel_id=1, source_target_pairs={{6,0},{0,8},{22,16},{16,24},{38,32},{32,40},{54,48},{48,56},{14,2}... | collective-permute-start | bytes 540680 | tf_op jit(solution)/shard_map/ppermute | solution.py:147
  285.8 24.1 %collective-permute-start.48 = (bf16[128,1024]{1,0:T(8,128)(2,1)S(1)}, bf16[128,1024]{1,0:T(8,128)(2,1)S(1)}, u32[]{:S(2)}, u32[]{:S(2)}) collective-permute-start(bf16[128,1024]{1,0:T(8,128)(2,1)S(1)} %get-tuple-element.106), channel_id=1, source_target_pairs={{0,64},{8,72},{16,80},{24,88},{32,96},{40,104},{48,112},{56,120},{... | collective-permute-start | bytes 786440 | tf_op jit(solution)/shard_map/ppermute | solution.py:46
  306.0 26.2 %collective-permute-start.58 = (bf16[1024,256]{1,0:T(8,128)(2,1)S(1)}, bf16[1024,256]{1,0:T(8,128)(2,1)S(1)}, u32[]{:S(2)}, u32[]{:S(2)}) collective-permute-start(bf16[1024,256]{1,0:T(8,128)(2,1)S(1)} %get-tuple-element.70), channel_id=1, source_target_pairs={{0,16},{8,24},{16,32},{24,40},{32,48},{40,56},{48,0},{56,8},{2,18}... | collective-permute-start | bytes 1572872 | tf_op jit(solution)/shard_map/ppermute | solution.py:46
  306.0 26.1 %collective-permute-start.59 = (bf16[1024,256]{1,0:T(8,128)(2,1)S(1)}, bf16[1024,256]{1,0:T(8,128)(2,1)S(1)}, u32[]{:S(2)}, u32[]{:S(2)}) collective-permute-start(bf16[1024,256]{1,0:T(8,128)(2,1)S(1)} %get-tuple-element.71), channel_id=1, source_target_pairs={{0,48},{8,56},{16,0},{24,8},{32,16},{40,24},{48,32},{56,40},{2,50}... | collective-permute-start | bytes 1572872 | tf_op jit(solution)/shard_map/ppermute | solution.py:46
  308.7 23.5 %collective-permute-start.60 = (bf16[1024,256]{1,0:T(8,128)(2,1)S(1)}, bf16[1024,256]{1,0:T(8,128)(2,1)S(1)}, u32[]{:S(2)}, u32[]{:S(2)}) collective-permute-start(bf16[1024,256]{1,0:T(8,128)(2,1)S(1)} %get-tuple-element.72), channel_id=1, source_target_pairs={{0,32},{8,40},{16,48},{24,56},{32,0},{40,8},{48,16},{56,24},{2,34}... | collective-permute-start | bytes 1572872 | tf_op jit(solution)/shard_map/ppermute | solution.py:46
  308.7 9.1 %collective-permute-start.50 = (bf16[128,1024]{1,0:T(8,128)(2,1)S(1)}, bf16[128,1024]{1,0:T(8,128)(2,1)S(1)}, u32[]{:S(2)}, u32[]{:S(2)}) collective-permute-start(bf16[128,1024]{1,0:T(8,128)(2,1)S(1)} %get-tuple-element.107), channel_id=1, source_target_pairs={{0,1},{8,9},{16,17},{24,25},{32,33},{40,41},{48,49},{56,57},{2,3},... | collective-permute-start | bytes 786440 | tf_op jit(solution)/shard_map/ppermute | solution.py:46
  309.9 12.7 %collective-permute-start.49 = (bf16[128,1024]{1,0:T(8,128)(2,1)S(1)}, bf16[128,1024]{1,0:T(8,128)(2,1)S(1)}, u32[]{:S(2)}, u32[]{:S(2)}) collective-permute-start(bf16[128,1024]{1,0:T(8,128)(2,1)S(1)} %get-tuple-element.108), channel_id=1, source_target_pairs={{0,65},{8,73},{16,81},{24,89},{32,97},{40,105},{48,113},{56,121},{... | collective-permute-start | bytes 786440 | tf_op jit(solution)/shard_map/ppermute | solution.py:46
  346.9 32.0 %collective-permute-start.61 = (bf16[512,1024]{1,0:T(8,128)(2,1)S(1)}, bf16[512,1024]{1,0:T(8,128)(2,1)S(1)}, u32[]{:S(2)}, u32[]{:S(2)}) collective-permute-start(bf16[512,1024]{1,0:T(8,128)(2,1)S(1)} %slice.164), channel_id=1, source_target_pairs={{0,8},{8,0},{16,24},{24,16},{32,40},{40,32},{48,56},{56,48},{2,10}... | collective-permute-start | bytes 3145736 | tf_op jit(solution)/shard_map/ppermute | solution.py:46
  359.5 9.3 %collective-permute-start.77 = (bf16[2,2,64,512]{3,2,1,0:T(8,128)(2,1)S(1)}, bf16[2,2,64,512]{3,2,1,0:T(8,128)(2,1)S(1)}, u32[]{:S(2)}, u32[]{:S(2)}) collective-permute-start(bf16[2,2,64,512]{3,2,1,0:T(8,128)(2,1)S(1)} %get-tuple-element.101), channel_id=1, source_target_pairs={{0,32},{8,40},{16,48},{24,56},{32,0},{40,8},{48,16},{56,24},{2,34}... | collective-permute-start | bytes 786440 | tf_op jit(solution)/shard_map/ppermute | solution.py:46
  360.2 8.6 %collective-permute-start.76 = (bf16[2,2,64,512]{3,2,1,0:T(8,128)(2,1)S(1)}, bf16[2,2,64,512]{3,2,1,0:T(8,128)(2,1)S(1)}, u32[]{:S(2)}, u32[]{:S(2)}) collective-permute-start(bf16[2,2,64,512]{3,2,1,0:T(8,128)(2,1)S(1)} %get-tuple-element.102), channel_id=1, source_target_pairs={{0,48},{8,56},{16,0},{24,8},{32,16},{40,24},{48,32},{56,40},{2,50}... | collective-permute-start | bytes 786440 | tf_op jit(solution)/shard_map/ppermute | solution.py:46
  368.9 12.8 %collective-permute-start.78 = (bf16[64,512]{1,0:T(8,128)(2,1)S(1)}, bf16[64,512]{1,0:T(8,128)(2,1)S(1)}, u32[]{:S(2)}, u32[]{:S(2)}) collective-permute-start(bf16[64,512]{1,0:T(8,128)(2,1)S(1)} %get-tuple-element.125), channel_id=1, source_target_pairs={{0,0},{2,8},{16,16},{18,24},{32,32},{34,40},{48,48},{50,56},{8,2},... | collective-permute-start | bytes 196616 | tf_op jit(solution)/shard_map/ppermute | solution.py:147
  376.5 8.3 %collective-permute-start.80 = (bf16[64,512]{1,0:T(8,128)(2,1)S(1)}, bf16[64,512]{1,0:T(8,128)(2,1)S(1)}, u32[]{:S(2)}, u32[]{:S(2)}) collective-permute-start(bf16[64,512]{1,0:T(8,128)(2,1)S(1)} %get-tuple-element.127), channel_id=1, source_target_pairs={{4,0},{6,8},{20,16},{22,24},{36,32},{38,40},{52,48},{54,56},{12,2}... | collective-permute-start | bytes 196616 | tf_op jit(solution)/shard_map/ppermute | solution.py:147
  379.4 8.5 %collective-permute-start.62 = (bf16[128,1024]{1,0:T(8,128)(2,1)S(1)}, bf16[128,1024]{1,0:T(8,128)(2,1)S(1)}, u32[]{:S(2)}, u32[]{:S(2)}) collective-permute-start(bf16[128,1024]{1,0:T(8,128)(2,1)S(1)} %get-tuple-element.103), channel_id=1, source_target_pairs={{0,64},{8,72},{16,80},{24,88},{32,96},{40,104},{48,112},{56,120},{... | collective-permute-start | bytes 786440 | tf_op jit(solution)/shard_map/ppermute | solution.py:46
  381.7 14.8 %collective-permute-start.64 = (bf16[128,1024]{1,0:T(8,128)(2,1)S(1)}, bf16[128,1024]{1,0:T(8,128)(2,1)S(1)}, u32[]{:S(2)}, u32[]{:S(2)}) collective-permute-start(bf16[128,1024]{1,0:T(8,128)(2,1)S(1)} %get-tuple-element.104), channel_id=1, source_target_pairs={{0,1},{8,9},{16,17},{24,25},{32,33},{40,41},{48,49},{56,57},{2,3},... | collective-permute-start | bytes 786440 | tf_op jit(solution)/shard_map/ppermute | solution.py:46
  384.1 12.5 %collective-permute-start.63 = (bf16[128,1024]{1,0:T(8,128)(2,1)S(1)}, bf16[128,1024]{1,0:T(8,128)(2,1)S(1)}, u32[]{:S(2)}, u32[]{:S(2)}) collective-permute-start(bf16[128,1024]{1,0:T(8,128)(2,1)S(1)} %get-tuple-element.105), channel_id=1, source_target_pairs={{0,65},{8,73},{16,81},{24,89},{32,97},{40,105},{48,113},{56,121},{... | collective-permute-start | bytes 786440 | tf_op jit(solution)/shard_map/ppermute | solution.py:46
  (56 other events, 521.0 us)
